TPU v7x, 32 devices: a whole 2x2x4 slice. The times are simulated.
32 devices in a mesh: item: 8 (over y, x, core), split: 4 (over z).
Axes of the slice: x: 2, y: 2, z: 4, core: 2. Of those that a mesh axis runs over, the one named last changes fastest.
Arguments:
- item_emb: float32 [4096, 128], P('item'), may hold values from -0.09375 to 0.09375
- confidences: bfloat16 [8, 4, 4, 16, 8, 128], P('item', 'split'), may hold values from 1 to 64
- user_block: int32 [8, 4, 4, 16], P('item', 'split'), may hold values from 0 to 2
- item_block: int32 [8, 4, 4, 16], P('item', 'split'), may hold values from 0 to 3
- block_age: int32 [8, 4, 4, 16], P('item', 'split'), may hold values from 0 to 15
- block_count: int32 [8, 4, 4], P('item', 'split'), may hold values from 8 to 16, as said below
Outputs:
- user_emb: float32 [192, 128], P('item')
Inputs may be any that keep to these rules, and one draw needn't show every extreme that they name: `block_count`: every device has 16 live slots at some window offset in some draw; some device has them in every draw.
All inputs are finite; a program needn't handle non-finite values.
Results may differ from a plain program's by a relative error of at most 0.0003.
Values sent between devices are 32-bit elements; how exact they have to be, the bound alone decides.
No kernel may reach another device: no remote copies, remote signals or barrier semaphores. Data moves between devices by JAX's collectives and lax.ppermute only.
A program may use at most 64 MiB of HBM per device.

v0:
```python
import jax
import jax.numpy as jnp
from jax import lax
from jax.sharding import PartitionSpec as P

USER_BLOCKS = 3
STEPS = 4
CG_ITERS = 3


ridge_weight = 0.1


def shifted(value, axis, steps):
    count = lax.axis_size(axis)
    pairs = [(source, (source + steps) % count) for source in range(count)]
    return lax.ppermute(value, axis, pairs)


def conjugate(matrix, right):
    solution = jnp.zeros_like(right)
    residual = right
    direction = right
    norm_now = jnp.sum(residual * residual, axis=1)
    for iteration in range(CG_ITERS):
        image = jnp.einsum("ude,ue->ud", matrix, direction, precision=lax.Precision.HIGHEST)
        step_size = norm_now / jnp.sum(direction * image, axis=1)
        solution = solution + step_size[:, None] * direction
        residual = residual - step_size[:, None] * image
        norm_next = jnp.sum(residual * residual, axis=1)
        direction = residual + (norm_next / norm_now)[:, None] * direction
        norm_now = norm_next
    return solution


def body(item_emb, confidences, user_block, item_block, block_age, block_count):
    features = item_emb.shape[1]
    block_users = confidences.shape[4]
    block_items = confidences.shape[5]
    users_dev = USER_BLOCKS * block_users

    def block_parts(current_rows, loop_step, position):
        user_start = user_block[0, 0, loop_step, position] * block_users
        item_start = item_block[0, 0, loop_step, position] * block_items
        recency = 2.0 / (2.0 + block_age[0, 0, loop_step, position].astype(jnp.float32))
        item_rows = lax.dynamic_slice_in_dim(current_rows, item_start, block_items, 0)
        weights = (
            lax.dynamic_index_in_dim(
                confidences[0, 0, loop_step], position, 0, keepdims=False
            ).astype(jnp.float32)
            * recency
        )
        return (user_start, recency, item_rows, weights)

    local_gram = jnp.dot(
        item_emb.T, item_emb, precision=lax.Precision.HIGHEST, preferred_element_type=jnp.float32
    )
    total_gram = lax.psum(local_gram, "item")
    base = total_gram + ridge_weight * jnp.eye(features, dtype=jnp.float32)
    window_shards = [item_emb]
    current_rows = item_emb
    for loop_step in range(1, STEPS):
        current_rows = shifted(current_rows, "item", 1)
        window_shards.append(current_rows)
    carried = (
        jnp.zeros((users_dev, features, features), jnp.float32),
        jnp.zeros((users_dev, features), jnp.float32),
    )
    for loop_step in range(STEPS):
        add_current_rows = window_shards[loop_step]

        def add_block(position, carried_now):
            user_gram, user_right = carried_now
            user_start, recency, item_rows, weights = block_parts(
                add_current_rows, loop_step, position
            )
            weighted = weights[:, None, :] * item_rows.T[None]
            correction = jnp.dot(
                weighted.reshape(block_users * features, block_items),
                item_rows,
                precision=lax.Precision.HIGHEST,
                preferred_element_type=jnp.float32,
            ).reshape(block_users, features, features)
            right_term = jnp.dot(
                weights + recency,
                item_rows,
                precision=lax.Precision.HIGHEST,
                preferred_element_type=jnp.float32,
            )
            old_gram = lax.dynamic_slice_in_dim(user_gram, user_start, block_users, 0)
            user_gram = lax.dynamic_update_slice_in_dim(
                user_gram, old_gram + correction, user_start, 0
            )
            old_right = lax.dynamic_slice_in_dim(user_right, user_start, block_users, 0)
            user_right = lax.dynamic_update_slice_in_dim(
                user_right, old_right + right_term, user_start, 0
            )
            return (user_gram, user_right)

        carried = lax.fori_loop(0, block_count[0, 0, loop_step], add_block, carried)
    user_gram, user_right = carried
    summed_gram, summed_right = lax.psum((user_gram, user_right), "split")
    solution = conjugate(summed_gram + base[None], summed_right)
    return solution


def solution(mesh):
    placed = (
        P("item", None),
        P("item", "split", None, None, None, None),
        P("item", "split", None, None),
        P("item", "split", None, None),
        P("item", "split", None, None),
        P("item", "split", None),
    )
    return jax.shard_map(
        body, mesh=mesh, in_specs=placed, out_specs=P("item", None), check_vma=False
    )
```

profile of v0, /device:TPU:0, one launch (start us, length us, event | category | flops | bytes accessed | tf_op | source)
XLA Modules:
  0.0 626.2 jit_solution(3849749117799046874)
XLA Ops:
  7.1 2.3 fusion.70
  9.4 1.5 fusion.69
  11.1 58.7 %while.48 = (s32[]{:T(128)}, f32[24,128,128]{2,1,0:T(8,128)S(1)}, f32[24,128]{1,0:T(8,128)S(1)}, s32[]{:T(128)}, s32[1,1,4,16]{3,2,1,0:T(4,128)S(1)}, /*index=5*...) while((s32[]{:T(128)}, f32[24,128,128]{2,1,0:T(8,128)S(1)}, ...), condition=%wide.region_1.2_spmd, body=%wide.region_0.0_spmd.sunk | while | flops 203167760 | bytes 1594699 | solution.py:100
  69.8 53.5 %collective-permute-start.1 = (f32[512,128]{1,0:T(8,128)}, f32[512,128]{1,0:T(8,128)}, u32[]{:S(2)}, u32[]{:S(2)}) collective-permute-start(f32[512,128]{1,0:T(8,128)} %collective-permute-done), channel_id=1, source_target_pairs={{0,4},{4,8},{8,12},{12,16},{16,20},{20,24},{24,28},{28,0},{1,5},{5... | collective-permute-start | bytes 786440 | tf_op jit(solution)/shard_map/ppermute | solution.py:17
  123.3 118.6 %while.49 = (s32[]{:T(128)}, f32[24,128,128]{2,1,0:T(8,128)S(1)}, f32[24,128]{1,0:T(8,128)S(1)}, s32[]{:T(128)}, s32[1,1,4,16]{3,2,1,0:T(4,128)S(1)}, /*index=5*...) while((s32[]{:T(128)}, f32[24,128,128]{2,1,0:T(8,128)S(1)}, ...), condition=%wide.region_3.4_spmd, body=%wide.region_2.3_spmd.sunk | while | flops 203167760 | bytes 1594699 | solution.py:100
  140.6 1.4 fusion.122
  150.4 1.4 fusion.122
  170.1 1.4 fusion.122
  189.7 1.4 fusion.122
  199.6 1.4 fusion.122
  219.2 1.4 fusion.122
  229.1 1.4 fusion.122
  242.0 146.4 %while.50 = (s32[]{:T(128)}, f32[24,128,128]{2,1,0:T(8,128)S(1)}, f32[24,128]{1,0:T(8,128)S(1)}, s32[]{:T(128)}, s32[1,1,4,16]{3,2,1,0:T(4,128)S(1)}, /*index=5*...) while((s32[]{:T(128)}, f32[24,128,128]{2,1,0:T(8,128)S(1)}, ...), condition=%wide.region_5.6_spmd, body=%wide.region_4.5_spmd.sunk | while | flops 203167760 | bytes 1594699 | solution.py:100
  249.3 1.4 fusion.130
  278.4 1.4 fusion.130
  317.3 1.4 fusion.130
  327.0 1.4 fusion.130
  346.4 1.4 fusion.130
  388.4 62.7 %while.51 = (s32[]{:T(128)}, f32[24,128,128]{2,1,0:T(8,128)S(1)}, f32[24,128]{1,0:T(8,128)S(1)}, s32[]{:T(128)}, s32[1,1,4,16]{3,2,1,0:T(4,128)S(1)}, /*index=5*...) while((s32[]{:T(128)}, f32[24,128,128]{2,1,0:T(8,128)S(1)}, ...), condition=%wide.region_7.8_spmd, body=%wide.region_6.7_spmd.sunk | while | flops 203167760 | bytes 1594699 | solution.py:100
  453.2 97.7 %psum.21 = f32[24,128]{1,0:T(8,128)S(1)} all-reduce(f32[24,128]{1,0:T(8,128)S(1)} %get-tuple-element.207), channel_id=1, replica_groups=mesh['item'=8,'split'=4] {'split'}, use_global_device_ids=true, to_apply=%region_8.9 | all-reduce | flops 3072 | bytes 24576 | tf_op jit(solution)/shard_map/psum | solution.py:102
  550.9 57.6 %all-reduce.3.cloned.1.call-done = f32[24,128,128]{2,1,0:T(8,128)} async-done(((f32[24,128,128]{2,1,0:T(8,128)}), f32[24,128,128]{2,1,0:T(8,128)}) %all-reduce.3.cloned.1.call-update) | async-done | bytes 1572880 | tf_op jit(solution)/shard_map/psum | solution.py:102
  608.6 4.1 fusion.52
  613.0 2.5 fusion.50
  616.0 2.5 fusion.48
  (380 shorter events, 148.3 us)
Async XLA Ops:
  6.5 4.5 copy-start.2
  6.5 4.5 copy-start.3
  6.5 4.5 copy-start.4
  6.5 4.6 copy-start.5
  6.5 4.6 copy-start.6
  6.5 445.8 %all-reduce.5.cloned.1.call-start = ((), (), s32[]{:S(2)}) async-start(), calls=%async_computation.1 | async-start | bytes 131072 | tf_op jit(solution)/shard_map/psum | solution.py:58
  6.6 63.2 %collective-permute-start = (f32[512,128]{1,0:T(8,128)}, f32[512,128]{1,0:T(8,128)}, u32[]{:S(2)}, u32[]{:S(2)}) collective-permute-start(f32[512,128]{1,0:T(8,128)} %param.14), channel_id=1, source_target_pairs={{0,4},{4,8},{8,12},{12,16},{16,20},{20,24},{24,28},{28,0},{1,5},{5... | collective-permute-start | bytes 786440 | tf_op jit(solution)/shard_map/ppermute | solution.py:17
  9.4 599.2 %all-reduce.3.cloned.1.call-start = ((), (), s32[]{:S(2)}) async-start(), calls=%async_computation | async-start | bytes 3145728 | tf_op jit(solution)/shard_map/psum | solution.py:102
  69.8 172.1 %collective-permute-start.1 = (f32[512,128]{1,0:T(8,128)}, f32[512,128]{1,0:T(8,128)}, u32[]{:S(2)}, u32[]{:S(2)}) collective-permute-start(f32[512,128]{1,0:T(8,128)} %collective-permute-done), channel_id=1, source_target_pairs={{0,4},{4,8},{8,12},{12,16},{16,20},{20,24},{24,28},{28,0},{1,5},{5... | collective-permute-start | bytes 786440 | tf_op jit(solution)/shard_map/ppermute | solution.py:17
  242.0 146.4 %collective-permute-start.2 = (f32[512,128]{1,0:T(8,128)}, f32[512,128]{1,0:T(8,128)S(1)}, u32[]{:S(2)}, u32[]{:S(2)}) collective-permute-start(f32[512,128]{1,0:T(8,128)} %collective-permute-done.1), channel_id=1, source_target_pairs={{0,4},{4,8},{8,12},{12,16},{16,20},{20,24},{24,28},{28,0},{1,5},{5... | collective-permute-start | bytes 786440 | tf_op jit(solution)/shard_map/ppermute | solution.py:17
  451.1 1.2 copy-start
  608.6 4.5 copy-start.1
Sparse Core Ops, SparseCore 0:
  10.4 55.2 all-reduce.4
  452.4 156.0 all-reduce.2
where the time goes:
time: 626 us
  loops' own time  226 us (36%)
  blocking collectives  97.7 us (16%)
  matrix products  89.1 us (14%)
  other arithmetic  58.3 us (9%)
  waiting for transfers between devices  57.7 us (9%)
  starting transfers between devices  54.2 us (9%)
  local copies, waits for them, and re-layouts  30 us (5%)
  between operations  13.6 us (2%)
    another operation x4, loops' own time, body(): carried = lax.fori_loop(0, block_count[0, 0, loop_step], add_block, carried)  226 us
    psum x1, blocking collectives, body(): summed_gram, summed_right = lax.psum((user_gram, user_right), 'split')  97.7 us
    psum x1, waiting for transfers between devices, body(): summed_gram, summed_right = lax.psum((user_gram, user_right), 'split')  57.6 us
    ppermute x3, starting transfers between devices, shifted(): return lax.ppermute(value, axis, pairs)  54.1 us
    dot_general x44, matrix products, add_block(): jnp.dot(weighted.reshape(block_users * features, block_items), item_rows,...  47.8 us
    dot_general x44, matrix products, add_block(): jnp.dot(weights + recency, item_rows, precision=lax.Precision.HIGHEST, pr...  29.9 us
    mul x44, other arithmetic, block_parts(): user_start = user_block[0, 0, loop_step, position] * block_users  27.9 us
    convert_element_type x44, other arithmetic, block_parts(): block_age[0, 0, loop_step, position].astype(jnp.float32)  27.3 us
  transfers between devices with their start and end apart: 5, of which 1 were waited for; matrix products, arithmetic and copies ran while one was open for 26% of the time, Pallas kernels for 0%

commit v1 on v0

v1 whole, which is shorter than its diff:
```python
import functools

import jax
import jax.numpy as jnp
from jax import lax
from jax.experimental import pallas as pl
from jax.experimental.pallas import tpu as pltpu
from jax.sharding import PartitionSpec as P

USER_BLOCKS = 3
STEPS = 4
CG_ITERS = 3
RIDGE = 0.1

SUB = 8
LANES = 128


def split_parts(value):
    high = value.astype(jnp.bfloat16).astype(jnp.float32)
    return high, value - high


def prepare_kernel(n_split, item_blocks, conf_tiles, gram_tiles, users, items, ages, counts, conf, emb, *rest):
    sends, gram_out, acc, gram = rest[:n_split], rest[n_split], rest[n_split + 1], rest[n_split + 2]
    cells = STEPS * item_blocks
    slots = conf.shape[3]
    z = lax.axis_index("split")
    odd = lax.rem(lax.axis_index("item"), 2)
    acc[...] = jnp.zeros_like(acc)
    lane = lax.broadcasted_iota(jnp.int32, (SUB, LANES), 1)
    recency_sums = jnp.zeros((SUB, LANES), jnp.float32)
    for k in range(STEPS):
        place = jnp.where(odd == 1, k, (STEPS - k) % STEPS)
        for j in range(slots):
            tile = users[0, 0, k, j] * cells + place * item_blocks + items[0, 0, k, j]
            age = jnp.full((SUB, LANES), ages[0, 0, k, j], jnp.int32).astype(jnp.float32)
            live = (j < counts[0, 0, k]).astype(jnp.float32)
            recency = 2.0 / (2.0 + age) * live
            acc[tile] = acc[tile] + conf[0, 0, k, j].astype(jnp.float32) * recency
            recency_sums = recency_sums + jnp.where(lane == tile, recency, 0.0)
    acc[USER_BLOCKS * cells] = recency_sums
    for s in range(n_split):
        chunk = lax.rem(z + s, n_split)
        sends[s][...] = acc[pl.ds(chunk * conf_tiles, conf_tiles)]

    value = emb[...]
    gram[...] = jnp.zeros_like(gram)
    product = lax.dot_general(
        value, value, (((0,), (0,)), ((), ())), precision=lax.Precision.HIGHEST, preferred_element_type=jnp.float32
    )
    gram[0 : LANES // SUB] = product.reshape(LANES // SUB, SUB, LANES)
    gram_out[...] = gram[pl.ds(z * gram_tiles, gram_tiles)]


def solve_kernel(n_split, item_blocks, conf_tiles, gram_tiles, *refs):
    shards = refs[:STEPS]
    chunks = refs[STEPS : STEPS + n_split]
    out, weights, gram, wide, tall = refs[STEPS + n_split :]
    cells = STEPS * item_blocks
    z = lax.axis_index("split")
    rows = shards[0].shape[0]
    users = USER_BLOCKS * SUB
    features = LANES

    for s in range(n_split):
        chunk = lax.rem(z + n_split - s, n_split)
        weights[pl.ds(chunk * conf_tiles, conf_tiles)] = chunks[s][0:conf_tiles]
        gram[pl.ds(chunk * gram_tiles, gram_tiles)] = chunks[s][conf_tiles : conf_tiles + gram_tiles]

    for k in range(STEPS):
        high, low = split_parts(shards[k][...])
        tall[k] = jnp.concatenate([high, low], axis=1).astype(jnp.bfloat16)
        wide[k] = jnp.concatenate([high.T, low.T], axis=0).astype(jnp.bfloat16)

    eye_rows = lax.broadcasted_iota(jnp.int32, (features, features), 0)
    eye_cols = lax.broadcasted_iota(jnp.int32, (features, features), 1)
    base = gram[0 : features // SUB].reshape(features, features) + jnp.where(eye_rows == eye_cols, RIDGE, 0.0)
    base_high, base_low = split_parts(base)
    base_pair = jnp.concatenate([base_high, base_low], axis=1).astype(jnp.bfloat16)

    def conf_of(k):
        return jnp.concatenate(
            [
                jnp.concatenate([weights[ub * cells + k * item_blocks + i] for i in range(item_blocks)], axis=1)
                for ub in range(USER_BLOCKS)
            ],
            axis=0,
        )

    recency_sums = weights[USER_BLOCKS * cells]

    def count_of(k):
        return jnp.concatenate(
            [
                jnp.concatenate(
                    [
                        jnp.broadcast_to(recency_sums[:, t : t + 1], (SUB, LANES))
                        for t in range(ub * cells + k * item_blocks, ub * cells + (k + 1) * item_blocks)
                    ],
                    axis=1,
                )
                for ub in range(USER_BLOCKS)
            ],
            axis=0,
        )

    def stacked(value):
        high, low = split_parts(value)
        return jnp.concatenate([high, low], axis=0).astype(jnp.bfloat16)

    def folded(pair):
        return (pair[:users, :features] + pair[:users, features:]) + (pair[users:, :features] + pair[users:, features:])

    def back(value, k):
        return jnp.dot(stacked(value), tall[k], preferred_element_type=jnp.float32)

    right = folded(sum(back(conf_of(k) + count_of(k), k) for k in range(STEPS)))

    def apply(direction):
        high, low = split_parts(direction)
        left = jnp.concatenate(
            [jnp.concatenate([high, high], axis=1), jnp.concatenate([low, low], axis=1)], axis=0
        ).astype(jnp.bfloat16)
        total = jnp.dot(left[:, :features], base_pair, preferred_element_type=jnp.float32)
        for k in range(STEPS):
            scores = jnp.dot(left, wide[k], preferred_element_type=jnp.float32)
            total = total + back((scores[:users] + scores[users:]) * conf_of(k), k)
        return folded(total)

    answer = jnp.zeros_like(right)
    residual = right
    direction = right
    norm_now = jnp.sum(residual * residual, axis=1, keepdims=True)
    for iteration in range(CG_ITERS):
        image = apply(direction)
        step = norm_now / jnp.sum(direction * image, axis=1, keepdims=True)
        answer = answer + step * direction
        if iteration + 1 < CG_ITERS:
            residual = residual - step * image
            norm_next = jnp.sum(residual * residual, axis=1, keepdims=True)
            direction = residual + (norm_next / norm_now) * direction
            norm_now = norm_next
    out[...] = answer


def body(item_emb, confidences, user_block, item_block, block_age, block_count):
    n_item, n_split = lax.axis_size("item"), lax.axis_size("split")
    rows, features = item_emb.shape
    block_users, block_items = confidences.shape[4:]
    item_blocks = rows // block_items
    tiles = USER_BLOCKS * STEPS * item_blocks + 1
    conf_tiles = pl.cdiv(tiles, n_split)
    gram_tiles = pl.cdiv(features // SUB, n_split)
    f32 = jnp.float32
    smem = pl.BlockSpec(memory_space=pltpu.SMEM)
    vmem = pl.BlockSpec(memory_space=pltpu.VMEM)

    def over_split(value, steps):
        return lax.ppermute(value, "split", [(i, (i + steps) % n_split) for i in range(n_split)])

    second = lax.ppermute(item_emb, "item", [(i, (i + 2) % n_item) for i in range(n_item)])
    first = lax.ppermute(item_emb, "item", [(i, (i + (3 if i % 2 else 1)) % n_item) for i in range(n_item)])
    third = lax.ppermute(second, "item", [(i, i ^ 1) for i in range(n_item)])

    prepared = pl.pallas_call(
        functools.partial(prepare_kernel, n_split, item_blocks, conf_tiles, gram_tiles),
        out_shape=[jax.ShapeDtypeStruct((conf_tiles, SUB, LANES), f32)] * n_split
        + [jax.ShapeDtypeStruct((gram_tiles, SUB, LANES), f32)],
        in_specs=[smem] * 4 + [vmem] * 2,
        out_specs=[vmem] * (n_split + 1),
        scratch_shapes=[
            pltpu.VMEM((n_split * conf_tiles, SUB, LANES), f32),
            pltpu.VMEM((n_split * gram_tiles, SUB, LANES), f32),
        ],
        name="prepare",
    )(user_block, item_block, block_age, block_count, confidences, item_emb)
    sends, gram = prepared[:n_split], prepared[n_split]

    distance = 1
    while distance < n_item:
        gram = gram + lax.ppermute(gram, "item", [(i, i ^ distance) for i in range(n_item)])
        distance *= 2
    mine = sends[0]
    for s in range(1, n_split):
        mine = mine + over_split(sends[s], s)
    mine = jnp.concatenate([mine, gram], axis=0)
    chunks = [mine] + [over_split(mine, s) for s in range(1, n_split)]

    return pl.pallas_call(
        functools.partial(solve_kernel, n_split, item_blocks, conf_tiles, gram_tiles),
        out_shape=jax.ShapeDtypeStruct((USER_BLOCKS * block_users, features), f32),
        in_specs=[vmem] * (STEPS + n_split),
        out_specs=vmem,
        scratch_shapes=[
            pltpu.VMEM((n_split * conf_tiles, SUB, LANES), f32),
            pltpu.VMEM((n_split * gram_tiles, SUB, LANES), f32),
            pltpu.VMEM((STEPS, 2 * features, rows), jnp.bfloat16),
            pltpu.VMEM((STEPS, rows, 2 * features), jnp.bfloat16),
        ],
        name="solve",
    )(item_emb, first, second, third, *chunks)


def solution(mesh):
    placed = (
        P("item", None),
        P("item", "split", None, None, None, None),
        P("item", "split", None, None),
        P("item", "split", None, None),
        P("item", "split", None, None),
        P("item", "split", None),
    )
    return jax.shard_map(
        body, mesh=mesh, in_specs=placed, out_specs=P("item", None), check_vma=False
    )
```

time: 626 us -> 37.2 us (0.06)
  loops' own time: 226 us -> 0 us
  blocking collectives: 97.7 us -> 0 us
  matrix products: 89.1 us -> 0 us
  other arithmetic: 58.3 us -> 0.76 us
  waiting for transfers between devices: 57.7 us -> 12.4 us
  starting transfers between devices: 54.2 us -> 15.6 us
  local copies, waits for them, and re-layouts: 30 us -> 1.41 us
  between operations: 13.6 us -> 0.11 us
  Pallas kernels: 0 us -> 6.73 us
    another operation x4 -> x0, loops' own time: 226 us -> none  [body(): carried = lax.fori_loop(0, block_count[0, 0, loop_step], add_block, carried)]
    psum x1 -> x0, blocking collectives: 97.7 us -> none  [body(): summed_gram, summed_right = lax.psum((user_gram, user_right), 'split')]
    dot_general x92 -> x0, matrix products: 89.1 us -> none  [the longest x44 47.8 us: add_block(): jnp.dot(weighted.reshape(block_users * features, block_items), item_rows,...]
    psum x2 -> x0, waiting for transfers between devices: 57.7 us -> none  [the longest x1 57.6 us: body(): summed_gram, summed_right = lax.psum((user_gram, user_right), 'split')]
    ppermute x3 -> x12, starting transfers between devices: 54.1 us -> 15.6 us  [the longest x6 7.92 us: over_split(): lax.ppermute(value, 'split', [(i, (i + steps) % n_split) for i in range(n...]
    mul x88 -> x0, other arithmetic: 28.5 us -> none  [the longest x44 27.9 us: block_parts(): user_start = user_block[0, 0, loop_step, position] * block_users]
    convert_element_type x44 -> x0, other arithmetic: 27.3 us -> none  [block_parts(): block_age[0, 0, loop_step, position].astype(jnp.float32)]
    transpose x88 -> x0, local copies, waits for them, and re-layouts: 27 us -> none  [add_block(): weighted = weights[:, None, :] * item_rows.T[None]]
  transfers between devices with their start and end apart: 5 -> 12, of which waited for: 1 -> 5; matrix products, arithmetic and copies ran while one was open for 26% -> 2% of each run, Pallas kernels for 0% -> 6%
where the time goes in v1:
time: 37.2 us; the launch traced here: 37 us
  starting transfers between devices  15.6 us (42%)
  waiting for transfers between devices  12.4 us (33%)
  Pallas kernels  6.73 us (18%)
  local copies, waits for them, and re-layouts  1.41 us (4%)
  other arithmetic  0.76 us (2%)
    ppermute x6, starting transfers between devices, over_split(): lax.ppermute(value, 'split', [(i, (i + steps) % n_split) for i in range(n...  7.92 us
    ppermute x6, waiting for transfers between devices, over_split(): lax.ppermute(value, 'split', [(i, (i + steps) % n_split) for i in range(n...  6.55 us
    ppermute x3, waiting for transfers between devices, body(): lax.ppermute(gram, 'item', [(i, i ^ distance) for i in range(n_item)])  5.85 us
    pallas_call x1, Pallas kernels, body(): pl.pallas_call(functools.partial(solve_kernel, n_split, item_blocks, conf...  4.54 us
    ppermute x3, starting transfers between devices, body(): lax.ppermute(gram, 'item', [(i, i ^ distance) for i in range(n_item)])  3.03 us
    ppermute x1, starting transfers between devices, body(): lax.ppermute(item_emb, 'item', [(i, (i + 2) % n_item) for i in range(n_it...  2.94 us
    pallas_call x1, Pallas kernels, body(): pl.pallas_call(functools.partial(prepare_kernel, n_split, item_blocks, co...  2.19 us
    ppermute x1, starting transfers between devices, body(): third = lax.ppermute(second, 'item', [(i, i ^ 1) for i in range(n_item)])  1.69 us
  transfers between devices with their start and end apart: 12, of which 5 were waited for; matrix products, arithmetic and copies ran while one was open for 2% of the time, Pallas kernels for 6%

profile of v1, /device:TPU:0, one launch (start us, length us, event | category | flops | bytes accessed | tf_op | source)
XLA Modules:
  0.0 37.0 jit_solution(14633941759033353861)
XLA Ops:
  0.0 2.9 %collective-permute-start.1 = (f32[512,128]{1,0:T(8,128)}, f32[512,128]{1,0:T(8,128)S(1)}, u32[]{:S(2)}, u32[]{:S(2)}) collective-permute-start(f32[512,128]{1,0:T(8,128)} %refs_0_.1), channel_id=1, source_target_pairs={{0,8},{4,12},{8,16},{12,20},{16,24},{20,28},{24,0},{28,4},{1,9},{5... | collective-permute-start | bytes 786440 | tf_op jit(solution)/shard_map/ppermute | solution.py:162
  2.9 2.2 %prepare.1 = (f32[13,8,128]{2,1,0:T(8,128)}, f32[13,8,128]{2,1,0:T(8,128)}, f32[13,8,128]{2,1,0:T(8,128)}, f32[13,8,128]{2,1,0:T(8,128)}, f32[4,8,128]{2,1,0:T(8,128)}) custom-call(s32[1,1,4,16]{3,2,1,0:T(4,128)} %users.1, s32[1,1,4,16]{3,2,1,0:T(4,128)} %items.1, s32[1,1,4,16]{3,2,1,0:T(4,128)} %ages.1, s32[1,1,4]{2,1,0:T(1,128)} %counts.1, ...), custom_call_target="tpu_custom_call" | custom-call | tf_op jit(solution)/shard_map/prepare/pallas_call | solution.py:166
  5.1 1.6 %collective-permute-start.3 = (f32[13,8,128]{2,1,0:T(8,128)}, f32[13,8,128]{2,1,0:T(8,128)S(1)}, u32[]{:S(2)}, u32[]{:S(2)}) collective-permute-start(f32[13,8,128]{2,1,0:T(8,128)} %get-tuple-element.11), channel_id=1, source_target_pairs={{0,1},{1,2},{2,3},{3,0},{4,5},{5,6},{6,7},{7,4},{8,9},{9,10},{10,1... | collective-permute-start | bytes 159752 | tf_op jit(solution)/shard_map/ppermute | solution.py:160
  6.7 2.6 %collective-permute-start.4 = (f32[13,8,128]{2,1,0:T(8,128)}, f32[13,8,128]{2,1,0:T(8,128)S(1)}, u32[]{:S(2)}, u32[]{:S(2)}) collective-permute-start(f32[13,8,128]{2,1,0:T(8,128)} %get-tuple-element.12), channel_id=1, source_target_pairs={{0,2},{1,3},{2,0},{3,1},{4,6},{5,7},{6,4},{7,5},{8,10},{9,11},{10,... | collective-permute-start | bytes 159752 | tf_op jit(solution)/shard_map/ppermute | solution.py:160
  9.3 1.3 %collective-permute-start.5 = (f32[13,8,128]{2,1,0:T(8,128)}, f32[13,8,128]{2,1,0:T(8,128)S(1)}, u32[]{:S(2)}, u32[]{:S(2)}) collective-permute-start(f32[13,8,128]{2,1,0:T(8,128)} %get-tuple-element.13), channel_id=1, source_target_pairs={{0,3},{1,0},{2,1},{3,2},{4,7},{5,4},{6,5},{7,6},{8,11},{9,8},{10,9... | collective-permute-start | bytes 159752 | tf_op jit(solution)/shard_map/ppermute | solution.py:160
  10.6 0.0 collective-permute-start.6
  10.6 1.4 %collective-permute-done.6 = f32[4,8,128]{2,1,0:T(8,128)S(1)} collective-permute-done((f32[4,8,128]{2,1,0:T(8,128)}, f32[4,8,128]{2,1,0:T(8,128)S(1)}, u32[]{:S(2)}, u32[]{:S(2)}) %collective-permute-start.6) | collective-permute-done | bytes 16416 | tf_op jit(solution)/shard_map/ppermute | solution.py:182
  12.0 0.7 %add.21 = f32[4,8,128]{2,1,0:T(8,128)S(1)} add(f32[4,8,128]{2,1,0:T(8,128)} %get-tuple-element.14, f32[4,8,128]{2,1,0:T(8,128)S(1)} %collective-permute-done.6) | non-fusion elementwise | flops 4096 | bytes 49152 | tf_op jit(solution)/shard_map/add | solution.py:182
  12.8 1.5 %collective-permute-start.7 = (f32[4,8,128]{2,1,0:T(8,128)S(1)}, f32[4,8,128]{2,1,0:T(8,128)S(1)}, u32[]{:S(2)}, u32[]{:S(2)}) collective-permute-start(f32[4,8,128]{2,1,0:T(8,128)S(1)} %add.21), channel_id=1, source_target_pairs={{0,8},{4,12},{8,0},{12,4},{16,24},{20,28},{24,16},{28,20},{1,9},{5... | collective-permute-start | bytes 49160 | tf_op jit(solution)/shard_map/ppermute | solution.py:182
  14.3 2.2 %collective-permute-done.7 = f32[4,8,128]{2,1,0:T(8,128)S(1)} collective-permute-done((f32[4,8,128]{2,1,0:T(8,128)S(1)}, f32[4,8,128]{2,1,0:T(8,128)S(1)}, u32[]{:S(2)}, u32[]{:S(2)}) %collective-permute-start.7) | collective-permute-done | bytes 16416 | tf_op jit(solution)/shard_map/ppermute | solution.py:182
  16.5 1.5 %collective-permute-start.8 = (f32[4,8,128]{2,1,0:T(8,128)S(1)}, f32[4,8,128]{2,1,0:T(8,128)S(1)}, u32[]{:S(2)}, u32[]{:S(2)}) collective-permute-start(f32[4,8,128]{2,1,0:T(8,128)S(1)} %add.22), channel_id=1, source_target_pairs={{0,16},{4,20},{8,24},{12,28},{16,0},{20,4},{24,8},{28,12},{1,17},{... | collective-permute-start | bytes 49160 | tf_op jit(solution)/shard_map/ppermute | solution.py:182
  18.0 2.2 %collective-permute-done.8 = f32[4,8,128]{2,1,0:T(8,128)S(1)} collective-permute-done((f32[4,8,128]{2,1,0:T(8,128)S(1)}, f32[4,8,128]{2,1,0:T(8,128)S(1)}, u32[]{:S(2)}, u32[]{:S(2)}) %collective-permute-start.8) | collective-permute-done | bytes 16416 | tf_op jit(solution)/shard_map/ppermute | solution.py:182
  20.2 0.0 collective-permute-start
  20.3 1.7 %collective-permute-start.2 = (f32[512,128]{1,0:T(8,128)S(1)}, f32[512,128]{1,0:T(8,128)S(1)}, u32[]{:S(2)}, u32[]{:S(2)}) collective-permute-start(f32[512,128]{1,0:T(8,128)S(1)} %collective-permute-done.1.refs_2_), channel_id=1, source_target_pairs={{0,4},{4,0},{8,12},{12,8},{16,20},{20,16},{24,28},{28,24},{1,5},{5... | collective-permute-start | bytes 786440 | tf_op jit(solution)/shard_map/ppermute | solution.py:164
  22.0 0.5 %collective-permute-start.11 = (f32[17,8,128]{2,1,0:T(8,128)S(1)}, f32[17,8,128]{2,1,0:T(8,128)S(1)}, u32[]{:S(2)}, u32[]{:S(2)}) collective-permute-start(f32[17,8,128]{2,1,0:T(8,128)S(1)} %pad_maximum_fusion.refs_4_), channel_id=1, source_target_pairs={{0,3},{1,0},{2,1},{3,2},{4,7},{5,4},{6,5},{7,6},{8,11},{9,8},{10,9... | collective-permute-start | bytes 208904 | tf_op jit(solution)/shard_map/ppermute | solution.py:160
  22.5 1.7 %collective-permute-start.10 = (f32[17,8,128]{2,1,0:T(8,128)S(1)}, f32[17,8,128]{2,1,0:T(8,128)S(1)}, u32[]{:S(2)}, u32[]{:S(2)}) collective-permute-start(f32[17,8,128]{2,1,0:T(8,128)S(1)} %pad_maximum_fusion.refs_4_), channel_id=1, source_target_pairs={{0,2},{1,3},{2,0},{3,1},{4,6},{5,7},{6,4},{7,5},{8,10},{9,11},{10,... | collective-permute-start | bytes 208904 | tf_op jit(solution)/shard_map/ppermute | solution.py:160
  24.2 0.2 collective-permute-start.9
  24.4 2.5 %collective-permute-done.11.refs_7_ = f32[17,8,128]{2,1,0:T(8,128)S(1)} collective-permute-done((f32[17,8,128]{2,1,0:T(8,128)S(1)}, f32[17,8,128]{2,1,0:T(8,128)S(1)}, u32[]{:S(2)}, u32[]{:S(2)}) %collective-permute-start.11) | collective-permute-done | bytes 69664 | tf_op jit(solution)/shard_map/ppermute | solution.py:160
  27.0 4.0 %collective-permute-done.10.refs_6_ = f32[17,8,128]{2,1,0:T(8,128)S(1)} collective-permute-done((f32[17,8,128]{2,1,0:T(8,128)S(1)}, f32[17,8,128]{2,1,0:T(8,128)S(1)}, u32[]{:S(2)}, u32[]{:S(2)}) %collective-permute-start.10) | collective-permute-done | bytes 69664 | tf_op jit(solution)/shard_map/ppermute | solution.py:160
  31.1 0.5 %copy-done.6 = f32[17,8,128]{2,1,0:T(8,128)} copy-done((f32[17,8,128]{2,1,0:T(8,128)}, f32[17,8,128]{2,1,0:T(8,128)S(1)}, u32[]{:S(2)}) %copy-start.6) | copy-done | bytes 69656
  31.6 0.0 copy-done.7
  31.6 0.1 copy-done.3
  31.7 0.7 %copy-done.4 = f32[512,128]{1,0:T(8,128)} copy-done((f32[512,128]{1,0:T(8,128)}, f32[512,128]{1,0:T(8,128)S(1)}, u32[]{:S(2)}) %copy-start.4) | copy-done | bytes 262168
  32.4 4.5 %solve.1 = f32[24,128]{1,0:T(8,128)} custom-call(f32[512,128]{1,0:T(8,128)} %refs_0_.1, f32[512,128]{1,0:T(8,128)} %copy-done.3, f32[512,128]{1,0:T(8,128)} %copy-done.2, f32[512,128]{1,0:T(8,128)} %copy-done.4, f32[17,8,128]{2,1,0:T(8,128)} %copy-done.1, f32[17,8,128]{2,1,0:T(8,128)} %copy-done.7, f32[17,8,128]{2,1,0:T(8,128)} %copy-done.6, ...), custom_call_target="tpu_custom_call" | custom-call | tf_op jit(solution)/shard_map/solve/pallas_call | solution.py:190
  (25 shorter events, 0.1 us)
Async XLA Ops:
  0.0 20.2 %copy-start = (f32[512,128]{1,0:T(8,128)S(1)}, f32[512,128]{1,0:T(8,128)}, u32[]{:S(2)}) copy-start(f32[512,128]{1,0:T(8,128)} %refs_0_.1) | copy-start | bytes 786436
  0.0 20.3 %collective-permute-start.1 = (f32[512,128]{1,0:T(8,128)}, f32[512,128]{1,0:T(8,128)S(1)}, u32[]{:S(2)}, u32[]{:S(2)}) collective-permute-start(f32[512,128]{1,0:T(8,128)} %refs_0_.1), channel_id=1, source_target_pairs={{0,8},{4,12},{8,16},{12,20},{16,24},{20,28},{24,0},{28,4},{1,9},{5... | collective-permute-start | bytes 786440 | tf_op jit(solution)/shard_map/ppermute | solution.py:162
  5.1 16.8 %collective-permute-start.3 = (f32[13,8,128]{2,1,0:T(8,128)}, f32[13,8,128]{2,1,0:T(8,128)S(1)}, u32[]{:S(2)}, u32[]{:S(2)}) collective-permute-start(f32[13,8,128]{2,1,0:T(8,128)} %get-tuple-element.11), channel_id=1, source_target_pairs={{0,1},{1,2},{2,3},{3,0},{4,5},{5,6},{6,7},{7,4},{8,9},{9,10},{10,1... | collective-permute-start | bytes 159752 | tf_op jit(solution)/shard_map/ppermute | solution.py:160
  6.7 15.3 %collective-permute-start.4 = (f32[13,8,128]{2,1,0:T(8,128)}, f32[13,8,128]{2,1,0:T(8,128)S(1)}, u32[]{:S(2)}, u32[]{:S(2)}) collective-permute-start(f32[13,8,128]{2,1,0:T(8,128)} %get-tuple-element.12), channel_id=1, source_target_pairs={{0,2},{1,3},{2,0},{3,1},{4,6},{5,7},{6,4},{7,5},{8,10},{9,11},{10,... | collective-permute-start | bytes 159752 | tf_op jit(solution)/shard_map/ppermute | solution.py:160
  9.3 12.7 %collective-permute-start.5 = (f32[13,8,128]{2,1,0:T(8,128)}, f32[13,8,128]{2,1,0:T(8,128)S(1)}, u32[]{:S(2)}, u32[]{:S(2)}) collective-permute-start(f32[13,8,128]{2,1,0:T(8,128)} %get-tuple-element.13), channel_id=1, source_target_pairs={{0,3},{1,0},{2,1},{3,2},{4,7},{5,4},{6,5},{7,6},{8,11},{9,8},{10,9... | collective-permute-start | bytes 159752 | tf_op jit(solution)/shard_map/ppermute | solution.py:160
  10.6 1.4 %collective-permute-start.6 = (f32[4,8,128]{2,1,0:T(8,128)}, f32[4,8,128]{2,1,0:T(8,128)S(1)}, u32[]{:S(2)}, u32[]{:S(2)}) collective-permute-start(f32[4,8,128]{2,1,0:T(8,128)} %get-tuple-element.14), channel_id=1, source_target_pairs={{0,4},{4,0},{8,12},{12,8},{16,20},{20,16},{24,28},{28,24},{1,5},{5... | collective-permute-start | bytes 49160 | tf_op jit(solution)/shard_map/ppermute | solution.py:182
  12.8 9.2 %copy-start.8 = (f32[13,8,128]{2,1,0:T(8,128)S(1)}, f32[13,8,128]{2,1,0:T(8,128)}, u32[]{:S(2)}) copy-start(f32[13,8,128]{2,1,0:T(8,128)} %get-tuple-element.10) | copy-start | bytes 159748
  12.8 3.7 %collective-permute-start.7 = (f32[4,8,128]{2,1,0:T(8,128)S(1)}, f32[4,8,128]{2,1,0:T(8,128)S(1)}, u32[]{:S(2)}, u32[]{:S(2)}) collective-permute-start(f32[4,8,128]{2,1,0:T(8,128)S(1)} %add.21), channel_id=1, source_target_pairs={{0,8},{4,12},{8,0},{12,4},{16,24},{20,28},{24,16},{28,20},{1,9},{5... | collective-permute-start | bytes 49160 | tf_op jit(solution)/shard_map/ppermute | solution.py:182
  16.5 3.7 %collective-permute-start.8 = (f32[4,8,128]{2,1,0:T(8,128)S(1)}, f32[4,8,128]{2,1,0:T(8,128)S(1)}, u32[]{:S(2)}, u32[]{:S(2)}) collective-permute-start(f32[4,8,128]{2,1,0:T(8,128)S(1)} %add.22), channel_id=1, source_target_pairs={{0,16},{4,20},{8,24},{12,28},{16,0},{20,4},{24,8},{28,12},{1,17},{... | collective-permute-start | bytes 49160 | tf_op jit(solution)/shard_map/ppermute | solution.py:182
  20.2 10.8 %collective-permute-start = (f32[512,128]{1,0:T(8,128)S(1)}, f32[512,128]{1,0:T(8,128)S(1)}, u32[]{:S(2)}, u32[]{:S(2)}) collective-permute-start(f32[512,128]{1,0:T(8,128)S(1)} %copy-done), channel_id=1, source_target_pairs={{0,4},{4,16},{8,12},{12,24},{16,20},{20,0},{24,28},{28,8},{1,5},{5... | collective-permute-start | bytes 786440 | tf_op jit(solution)/shard_map/ppermute | solution.py:163
  20.3 10.8 %copy-start.2 = (f32[512,128]{1,0:T(8,128)}, f32[512,128]{1,0:T(8,128)S(1)}, u32[]{:S(2)}) copy-start(f32[512,128]{1,0:T(8,128)S(1)} %collective-permute-done.1.refs_2_) | copy-start | bytes 786436
  20.3 10.7 %collective-permute-start.2 = (f32[512,128]{1,0:T(8,128)S(1)}, f32[512,128]{1,0:T(8,128)S(1)}, u32[]{:S(2)}, u32[]{:S(2)}) collective-permute-start(f32[512,128]{1,0:T(8,128)S(1)} %collective-permute-done.1.refs_2_), channel_id=1, source_target_pairs={{0,4},{4,0},{8,12},{12,8},{16,20},{20,16},{24,28},{28,24},{1,5},{5... | collective-permute-start | bytes 786440 | tf_op jit(solution)/shard_map/ppermute | solution.py:164
  22.0 9.0 %copy-start.1 = (f32[17,8,128]{2,1,0:T(8,128)}, f32[17,8,128]{2,1,0:T(8,128)S(1)}, u32[]{:S(2)}) copy-start(f32[17,8,128]{2,1,0:T(8,128)S(1)} %pad_maximum_fusion.refs_4_) | copy-start | bytes 208900
  22.0 4.9 %collective-permute-start.11 = (f32[17,8,128]{2,1,0:T(8,128)S(1)}, f32[17,8,128]{2,1,0:T(8,128)S(1)}, u32[]{:S(2)}, u32[]{:S(2)}) collective-permute-start(f32[17,8,128]{2,1,0:T(8,128)S(1)} %pad_maximum_fusion.refs_4_), channel_id=1, source_target_pairs={{0,3},{1,0},{2,1},{3,2},{4,7},{5,4},{6,5},{7,6},{8,11},{9,8},{10,9... | collective-permute-start | bytes 208904 | tf_op jit(solution)/shard_map/ppermute | solution.py:160
  22.5 8.5 %collective-permute-start.10 = (f32[17,8,128]{2,1,0:T(8,128)S(1)}, f32[17,8,128]{2,1,0:T(8,128)S(1)}, u32[]{:S(2)}, u32[]{:S(2)}) collective-permute-start(f32[17,8,128]{2,1,0:T(8,128)S(1)} %pad_maximum_fusion.refs_4_), channel_id=1, source_target_pairs={{0,2},{1,3},{2,0},{3,1},{4,6},{5,7},{6,4},{7,5},{8,10},{9,11},{10,... | collective-permute-start | bytes 208904 | tf_op jit(solution)/shard_map/ppermute | solution.py:160
  24.2 6.8 %collective-permute-start.9 = (f32[17,8,128]{2,1,0:T(8,128)S(1)}, f32[17,8,128]{2,1,0:T(8,128)S(1)}, u32[]{:S(2)}, u32[]{:S(2)}) collective-permute-start(f32[17,8,128]{2,1,0:T(8,128)S(1)} %pad_maximum_fusion.refs_4_), channel_id=1, source_target_pairs={{0,1},{1,2},{2,3},{3,0},{4,5},{5,6},{6,7},{7,4},{8,9},{9,10},{10,1... | collective-permute-start | bytes 208904 | tf_op jit(solution)/shard_map/ppermute | solution.py:160
  27.0 4.1 %copy-start.5 = (f32[17,8,128]{2,1,0:T(8,128)}, f32[17,8,128]{2,1,0:T(8,128)S(1)}, u32[]{:S(2)}) copy-start(f32[17,8,128]{2,1,0:T(8,128)S(1)} %collective-permute-done.11.refs_7_) | copy-start | bytes 208900
  31.0 0.6 %copy-start.6 = (f32[17,8,128]{2,1,0:T(8,128)}, f32[17,8,128]{2,1,0:T(8,128)S(1)}, u32[]{:S(2)}) copy-start(f32[17,8,128]{2,1,0:T(8,128)S(1)} %collective-permute-done.10.refs_6_) | copy-start | bytes 208900
  31.0 0.6 %copy-start.7 = (f32[17,8,128]{2,1,0:T(8,128)}, f32[17,8,128]{2,1,0:T(8,128)S(1)}, u32[]{:S(2)}) copy-start(f32[17,8,128]{2,1,0:T(8,128)S(1)} %collective-permute-done.9.refs_5_) | copy-start | bytes 208900
  31.0 0.7 %copy-start.3 = (f32[512,128]{1,0:T(8,128)}, f32[512,128]{1,0:T(8,128)S(1)}, u32[]{:S(2)}) copy-start(f32[512,128]{1,0:T(8,128)S(1)} %collective-permute-done.refs_1_) | copy-start | bytes 786436
  31.7 0.7 %copy-start.4 = (f32[512,128]{1,0:T(8,128)}, f32[512,128]{1,0:T(8,128)S(1)}, u32[]{:S(2)}) copy-start(f32[512,128]{1,0:T(8,128)S(1)} %collective-permute-done.2.refs_3_) | copy-start | bytes 786436

commit v2 on v1

--- a/solution.py
+++ b/solution.py
@@ -11,6 +11,7 @@
 STEPS = 4
 CG_ITERS = 3
 RIDGE = 0.1
+VMEM_LIMIT = 16 * 2**20
 
 SUB = 8
 LANES = 128
@@ -21,13 +22,19 @@
     return high, value - high
 
 
-def prepare_kernel(n_split, item_blocks, conf_tiles, gram_tiles, users, items, ages, counts, conf, emb, *rest):
-    sends, gram_out, acc, gram = rest[:n_split], rest[n_split], rest[n_split + 1], rest[n_split + 2]
+def weights_kernel(item_blocks, half, *refs):
+    arrays, (keep, send), held, (acc, arrived) = refs[:5], refs[5:7], refs[7:12], refs[12:]
+    copies = [pltpu.make_async_copy(a, h, arrived.at[i]) for i, (a, h) in enumerate(zip(arrays, held))]
+    for copy in copies:
+        copy.start()
+    acc[...] = jnp.zeros_like(acc)
+    for copy in copies:
+        copy.wait()
+    users, items, ages, counts, conf = held
     cells = STEPS * item_blocks
     slots = conf.shape[3]
-    z = lax.axis_index("split")
+    upper = lax.rem(lax.axis_index("split"), 2)
     odd = lax.rem(lax.axis_index("item"), 2)
-    acc[...] = jnp.zeros_like(acc)
     lane = lax.broadcasted_iota(jnp.int32, (SUB, LANES), 1)
     recency_sums = jnp.zeros((SUB, LANES), jnp.float32)
     for k in range(STEPS):
@@ -40,33 +47,27 @@
             acc[tile] = acc[tile] + conf[0, 0, k, j].astype(jnp.float32) * recency
             recency_sums = recency_sums + jnp.where(lane == tile, recency, 0.0)
     acc[USER_BLOCKS * cells] = recency_sums
-    for s in range(n_split):
-        chunk = lax.rem(z + s, n_split)
-        sends[s][...] = acc[pl.ds(chunk * conf_tiles, conf_tiles)]
-
+    keep[...] = acc[pl.ds(upper * half, half)]
+    send[...] = acc[pl.ds((1 - upper) * half, half)]
+
+
+def gram_kernel(emb, out):
     value = emb[...]
-    gram[...] = jnp.zeros_like(gram)
-    product = lax.dot_general(
+    out[...] = lax.dot_general(
         value, value, (((0,), (0,)), ((), ())), precision=lax.Precision.HIGHEST, preferred_element_type=jnp.float32
     )
-    gram[0 : LANES // SUB] = product.reshape(LANES // SUB, SUB, LANES)
-    gram_out[...] = gram[pl.ds(z * gram_tiles, gram_tiles)]
-
-
-def solve_kernel(n_split, item_blocks, conf_tiles, gram_tiles, *refs):
+
+
+def solve_kernel(item_blocks, half, *refs):
     shards = refs[:STEPS]
-    chunks = refs[STEPS : STEPS + n_split]
-    out, weights, gram, wide, tall = refs[STEPS + n_split :]
+    gram, keep, other, out, weights, wide, tall = refs[STEPS:]
     cells = STEPS * item_blocks
-    z = lax.axis_index("split")
-    rows = shards[0].shape[0]
+    upper = lax.rem(lax.axis_index("split"), 2)
     users = USER_BLOCKS * SUB
     features = LANES
 
-    for s in range(n_split):
-        chunk = lax.rem(z + n_split - s, n_split)
-        weights[pl.ds(chunk * conf_tiles, conf_tiles)] = chunks[s][0:conf_tiles]
-        gram[pl.ds(chunk * gram_tiles, gram_tiles)] = chunks[s][conf_tiles : conf_tiles + gram_tiles]
+    weights[pl.ds(upper * half, half)] = keep[...]
+    weights[pl.ds((1 - upper) * half, half)] = other[...]
 
     for k in range(STEPS):
         high, low = split_parts(shards[k][...])
@@ -75,7 +76,7 @@
 
     eye_rows = lax.broadcasted_iota(jnp.int32, (features, features), 0)
     eye_cols = lax.broadcasted_iota(jnp.int32, (features, features), 1)
-    base = gram[0 : features // SUB].reshape(features, features) + jnp.where(eye_rows == eye_cols, RIDGE, 0.0)
+    base = gram[...] + jnp.where(eye_rows == eye_cols, RIDGE, 0.0)
     base_high, base_low = split_parts(base)
     base_pair = jnp.concatenate([base_high, base_low], axis=1).astype(jnp.bfloat16)
 
@@ -149,57 +150,73 @@
     rows, features = item_emb.shape
     block_users, block_items = confidences.shape[4:]
     item_blocks = rows // block_items
-    tiles = USER_BLOCKS * STEPS * item_blocks + 1
-    conf_tiles = pl.cdiv(tiles, n_split)
-    gram_tiles = pl.cdiv(features // SUB, n_split)
+    half = pl.cdiv(USER_BLOCKS * STEPS * item_blocks + 1, 2)
     f32 = jnp.float32
-    smem = pl.BlockSpec(memory_space=pltpu.SMEM)
+    hbm = pl.BlockSpec(memory_space=pltpu.HBM)
     vmem = pl.BlockSpec(memory_space=pltpu.VMEM)
-
-    def over_split(value, steps):
-        return lax.ppermute(value, "split", [(i, (i + steps) % n_split) for i in range(n_split)])
-
-    second = lax.ppermute(item_emb, "item", [(i, (i + 2) % n_item) for i in range(n_item)])
-    first = lax.ppermute(item_emb, "item", [(i, (i + (3 if i % 2 else 1)) % n_item) for i in range(n_item)])
-    third = lax.ppermute(second, "item", [(i, i ^ 1) for i in range(n_item)])
-
-    prepared = pl.pallas_call(
-        functools.partial(prepare_kernel, n_split, item_blocks, conf_tiles, gram_tiles),
-        out_shape=[jax.ShapeDtypeStruct((conf_tiles, SUB, LANES), f32)] * n_split
-        + [jax.ShapeDtypeStruct((gram_tiles, SUB, LANES), f32)],
-        in_specs=[smem] * 4 + [vmem] * 2,
-        out_specs=[vmem] * (n_split + 1),
-        scratch_shapes=[
-            pltpu.VMEM((n_split * conf_tiles, SUB, LANES), f32),
-            pltpu.VMEM((n_split * gram_tiles, SUB, LANES), f32),
+    params = pltpu.CompilerParams(vmem_limit_bytes=VMEM_LIMIT)
+    half_tiles = jax.ShapeDtypeStruct((half, SUB, LANES), f32)
+
+    def pair(value, axis):
+        return lax.ppermute(value, axis, [(i, i ^ 1) for i in range(lax.axis_size(axis))])
+
+    def shifted(value, axis, steps):
+        count = lax.axis_size(axis)
+        return lax.ppermute(value, axis, [(i, (i + steps) % count) for i in range(count)])
+
+    slot_arrays = (user_block, item_block, block_age, block_count)
+    keep, send = pl.pallas_call(
+        functools.partial(weights_kernel, item_blocks, half),
+        out_shape=[half_tiles, half_tiles],
+        in_specs=[hbm] * 5,
+        out_specs=[vmem] * 2,
+        scratch_shapes=[pltpu.SMEM(a.shape, a.dtype) for a in slot_arrays]
+        + [
+            pltpu.VMEM(confidences.shape, confidences.dtype),
+            pltpu.VMEM((2 * half, SUB, LANES), f32),
+            pltpu.SemaphoreType.DMA((5,)),
         ],
-        name="prepare",
-    )(user_block, item_block, block_age, block_count, confidences, item_emb)
-    sends, gram = prepared[:n_split], prepared[n_split]
-
-    distance = 1
-    while distance < n_item:
-        gram = gram + lax.ppermute(gram, "item", [(i, i ^ distance) for i in range(n_item)])
-        distance *= 2
-    mine = sends[0]
-    for s in range(1, n_split):
-        mine = mine + over_split(sends[s], s)
-    mine = jnp.concatenate([mine, gram], axis=0)
-    chunks = [mine] + [over_split(mine, s) for s in range(1, n_split)]
+        compiler_params=params,
+        name="weights",
+    )(*[pltpu.with_memory_space_constraint(a, pltpu.HBM) for a in (*slot_arrays, confidences)])
+    keep = keep + pair(send, "split")
+
+    second, sent = lax.optimization_barrier((shifted(item_emb, "item", 2), item_emb))
+    first = lax.ppermute(sent, "item", [(i, (i + (3 if i % 2 else 1)) % n_item) for i in range(n_item)])
+    third = pair(second, "item")
+
+    gram = pl.pallas_call(
+        gram_kernel,
+        out_shape=jax.ShapeDtypeStruct((features, features), f32),
+        in_specs=[vmem],
+        out_specs=vmem,
+        compiler_params=params,
+        name="gram",
+    )(item_emb)
+    chip_gram = gram + pair(gram, "item")
+    keep, chip_gram = lax.optimization_barrier((keep, chip_gram))
+    gram = chip_gram
+    for steps in range(2, n_item, 2):
+        gram = gram + shifted(chip_gram, "item", steps)
+
+    total = keep
+    for steps in range(2, n_split, 2):
+        total = total + shifted(keep, "split", steps)
+    other = pair(total, "split")
 
     return pl.pallas_call(
-        functools.partial(solve_kernel, n_split, item_blocks, conf_tiles, gram_tiles),
+        functools.partial(solve_kernel, item_blocks, half),
         out_shape=jax.ShapeDtypeStruct((USER_BLOCKS * block_users, features), f32),
-        in_specs=[vmem] * (STEPS + n_split),
+        in_specs=[vmem] * (STEPS + 3),
         out_specs=vmem,
         scratch_shapes=[
-            pltpu.VMEM((n_split * conf_tiles, SUB, LANES), f32),
-            pltpu.VMEM((n_split * gram_tiles, SUB, LANES), f32),
+            pltpu.VMEM((2 * half, SUB, LANES), f32),
             pltpu.VMEM((STEPS, 2 * features, rows), jnp.bfloat16),
             pltpu.VMEM((STEPS, rows, 2 * features), jnp.bfloat16),
         ],
+        compiler_params=params,
         name="solve",
-    )(item_emb, first, second, third, *chunks)
+    )(item_emb, first, second, third, gram, total, other)
 
 
 def solution(mesh):

time: 37.2 us -> 25.5 us (0.69)
  waiting for transfers between devices: 12.4 us -> 7.12 us
  starting transfers between devices: 15.6 us -> 12.2 us
  Pallas kernels: 6.73 us -> 5 us
  other arithmetic: 0.76 us -> 0.06 us
  local copies, waits for them, and re-layouts: 1.41 us -> 0.95 us
    ppermute x12 -> x10, waiting for transfers between devices: 12.4 us -> 7.12 us  [the longest x4 3.77 us: pair(): lax.ppermute(value, axis, [(i, i ^ 1) for i in range(lax.axis_size(axis))])]
    ppermute x12 -> x10, starting transfers between devices: 15.6 us -> 12.2 us  [the longest x5 9.13 us: shifted(): lax.ppermute(value, axis, [(i, (i + steps) % count) for i in range(count)])]
    pallas_call x2 -> x3, Pallas kernels: 6.73 us -> 5 us  [the longest x1 3.3 us: body(): pl.pallas_call(functools.partial(solve_kernel, item_blocks, half), out_sh...]
    add x4, other arithmetic: 0.75 us -> 0.06 us  [the longest x1 0.02 us: body(): gram = gram + shifted(chip_gram, 'item', steps)]
    unnamed x18 -> x2, local copies, waits for them, and re-layouts: 1.41 us -> 0.95 us
  transfers between devices with their start and end apart: 12 -> 10, of which waited for: 5 -> 6; matrix products, arithmetic and copies ran while one was open for 2% -> 0% of each run, Pallas kernels for 6% -> 7%
where the time goes in v2:
time: 25.5 us; the launch traced here: 25.3 us
  starting transfers between devices  12.2 us (48%)
  waiting for transfers between devices  7.12 us (28%)
  Pallas kernels  5 us (20%)
  local copies, waits for them, and re-layouts  0.95 us (4%)
    ppermute x5, starting transfers between devices, shifted(): lax.ppermute(value, axis, [(i, (i + steps) % count) for i in range(count)])  9.13 us
    ppermute x4, waiting for transfers between devices, pair(): lax.ppermute(value, axis, [(i, i ^ 1) for i in range(lax.axis_size(axis))])  3.77 us
    ppermute x5, waiting for transfers between devices, shifted(): lax.ppermute(value, axis, [(i, (i + steps) % count) for i in range(count)])  3.36 us
    pallas_call x1, Pallas kernels, body(): pl.pallas_call(functools.partial(solve_kernel, item_blocks, half), out_sh...  3.3 us
    ppermute x4, starting transfers between devices, pair(): lax.ppermute(value, axis, [(i, i ^ 1) for i in range(lax.axis_size(axis))])  3.01 us
    pallas_call x1, Pallas kernels, body(): pl.pallas_call(functools.partial(weights_kernel, item_blocks, half), out_...  1.28 us
    unnamed x2, local copies, waits for them, and re-layouts  0.95 us
  transfers between devices with their start and end apart: 10, of which 6 were waited for; matrix products, arithmetic and copies ran while one was open for 0% of the time, Pallas kernels for 7%

profile of v2, /device:TPU:0, one launch (start us, length us, event | category | flops | bytes accessed | tf_op | source)
XLA Modules:
  0.0 25.3 jit_solution(1884398290330781622)
XLA Ops:
  0.0 2.9 %collective-permute-start = (f32[512,128]{1,0:T(8,128)}, f32[512,128]{1,0:T(8,128)S(1)}, u32[]{:S(2)}, u32[]{:S(2)}) collective-permute-start(f32[512,128]{1,0:T(8,128)} %refs_0_.3), channel_id=1, source_target_pairs={{0,8},{4,12},{8,16},{12,20},{16,24},{20,28},{24,0},{28,4},{1,9},{5... | collective-permute-start | bytes 786440 | tf_op jit(solution)/shard_map/ppermute | solution.py:165
  2.9 1.3 %weights.1 = (f32[25,8,128]{2,1,0:T(8,128)S(1)}, f32[25,8,128]{2,1,0:T(8,128)S(1)}) custom-call(s32[1,1,4,16]{3,2,1,0:T(4,128)} %refs_0_.2, s32[1,1,4,16]{3,2,1,0:T(4,128)} %refs_1_.1, s32[1,1,4,16]{3,2,1,0:T(4,128)} %refs_2_.1, s32[1,1,4]{2,1,0:T(1,128)} %refs_3_.1, bf16[1,1,4,16,8,128]{5,4,3,2,1,0:T(8,128)(2,1)} %refs_4_.1), custom_call_target="tpu_custom_call" | custom-call | tf_op jit(solution)/shard_map/weights/pallas_call | solution.py:168
  4.2 1.6 %collective-permute-start.3 = (f32[25,8,128]{2,1,0:T(8,128)S(1)}, f32[25,8,128]{2,1,0:T(8,128)S(1)}, u32[]{:S(2)}, u32[]{:S(2)}) collective-permute-start(f32[25,8,128]{2,1,0:T(8,128)S(1)} %get-tuple-element.14), channel_id=1, source_target_pairs={{0,1},{1,0},{2,3},{3,2},{4,5},{5,4},{6,7},{7,6},{8,9},{9,8},{10,11... | collective-permute-start | bytes 307208 | tf_op jit(solution)/shard_map/ppermute | solution.py:161
  5.9 0.9 %copy-done = f32[512,128]{1,0:T(8,128)S(1)} copy-done((f32[512,128]{1,0:T(8,128)S(1)}, f32[512,128]{1,0:T(8,128)}, u32[]{:S(2)}) %copy-start) | copy-done | bytes 262168
  6.8 0.4 %gram.1 = f32[128,128]{1,0:T(8,128)S(1)} custom-call(f32[512,128]{1,0:T(8,128)S(1)} %copy-done), custom_call_target="tpu_custom_call" | custom-call | tf_op jit(solution)/shard_map/gram/pallas_call | solution.py:188
  7.2 0.1 collective-permute-start.4
  7.3 1.2 %collective-permute-done.4 = f32[128,128]{1,0:T(8,128)S(1)} collective-permute-done((f32[128,128]{1,0:T(8,128)S(1)}, f32[128,128]{1,0:T(8,128)S(1)}, u32[]{:S(2)}, u32[]{:S(2)}) %collective-permute-start.4) | collective-permute-done | bytes 65568 | tf_op jit(solution)/shard_map/ppermute | solution.py:161
  8.6 0.4 %collective-permute-done.3 = f32[25,8,128]{2,1,0:T(8,128)S(1)} collective-permute-done((f32[25,8,128]{2,1,0:T(8,128)S(1)}, f32[25,8,128]{2,1,0:T(8,128)S(1)}, u32[]{:S(2)}, u32[]{:S(2)}) %collective-permute-start.3) | collective-permute-done | bytes 102432 | tf_op jit(solution)/shard_map/ppermute | solution.py:161
  9.0 2.7 %collective-permute-start.8 = (f32[25,8,128]{2,1,0:T(8,128)S(1)}, f32[25,8,128]{2,1,0:T(8,128)S(1)}, u32[]{:S(2)}, u32[]{:S(2)}) collective-permute-start(f32[25,8,128]{2,1,0:T(8,128)S(1)} %add.18), channel_id=1, source_target_pairs={{0,2},{1,3},{2,0},{3,1},{4,6},{5,7},{6,4},{7,5},{8,10},{9,11},{10,... | collective-permute-start | bytes 307208 | tf_op jit(solution)/shard_map/ppermute | solution.py:165
  11.6 1.4 %collective-permute-start.7 = (f32[128,128]{1,0:T(8,128)S(1)}, f32[128,128]{1,0:T(8,128)S(1)}, u32[]{:S(2)}, u32[]{:S(2)}) collective-permute-start(f32[128,128]{1,0:T(8,128)S(1)} %add.19), channel_id=1, source_target_pairs={{0,24},{4,28},{8,0},{12,4},{16,8},{20,12},{24,16},{28,20},{1,25},{... | collective-permute-start | bytes 196616 | tf_op jit(solution)/shard_map/ppermute | solution.py:165
  13.1 1.5 %collective-permute-start.6 = (f32[128,128]{1,0:T(8,128)S(1)}, f32[128,128]{1,0:T(8,128)S(1)}, u32[]{:S(2)}, u32[]{:S(2)}) collective-permute-start(f32[128,128]{1,0:T(8,128)S(1)} %add.19), channel_id=1, source_target_pairs={{0,16},{4,20},{8,24},{12,28},{16,0},{20,4},{24,8},{28,12},{1,17},{... | collective-permute-start | bytes 196616 | tf_op jit(solution)/shard_map/ppermute | solution.py:165
  14.6 0.6 %collective-permute-start.5 = (f32[128,128]{1,0:T(8,128)S(1)}, f32[128,128]{1,0:T(8,128)S(1)}, u32[]{:S(2)}, u32[]{:S(2)}) collective-permute-start(f32[128,128]{1,0:T(8,128)S(1)} %add.19), channel_id=1, source_target_pairs={{0,8},{4,12},{8,16},{12,20},{16,24},{20,28},{24,0},{28,4},{1,9},{5... | collective-permute-start | bytes 196616 | tf_op jit(solution)/shard_map/ppermute | solution.py:165
  15.2 0.0 collective-permute-done.refs_2_
  15.2 0.0 collective-permute-start.1
  15.2 1.5 %collective-permute-done.8 = f32[25,8,128]{2,1,0:T(8,128)S(1)} collective-permute-done((f32[25,8,128]{2,1,0:T(8,128)S(1)}, f32[25,8,128]{2,1,0:T(8,128)S(1)}, u32[]{:S(2)}, u32[]{:S(2)}) %collective-permute-start.8) | collective-permute-done | bytes 102432 | tf_op jit(solution)/shard_map/ppermute | solution.py:165
  16.6 0.0 collective-permute-start.2
  16.7 0.0 collective-permute-done.7
  16.7 1.3 %collective-permute-start.9 = (f32[25,8,128]{2,1,0:T(8,128)S(1)}, f32[25,8,128]{2,1,0:T(8,128)S(1)}, u32[]{:S(2)}, u32[]{:S(2)}) collective-permute-start(f32[25,8,128]{2,1,0:T(8,128)S(1)} %add.23.refs_5_), channel_id=1, source_target_pairs={{0,1},{1,0},{2,3},{3,2},{4,5},{5,4},{6,7},{7,6},{8,9},{9,8},{10,11... | collective-permute-start | bytes 307208 | tf_op jit(solution)/shard_map/ppermute | solution.py:161
  18.0 0.1 collective-permute-done.6
  18.0 1.8 %collective-permute-done.5 = f32[128,128]{1,0:T(8,128)S(1)} collective-permute-done((f32[128,128]{1,0:T(8,128)S(1)}, f32[128,128]{1,0:T(8,128)S(1)}, u32[]{:S(2)}, u32[]{:S(2)}) %collective-permute-start.5) | collective-permute-done | bytes 65568 | tf_op jit(solution)/shard_map/ppermute | solution.py:165
  19.9 2.1 %collective-permute-done.9.refs_6_ = f32[25,8,128]{2,1,0:T(8,128)S(1)} collective-permute-done((f32[25,8,128]{2,1,0:T(8,128)S(1)}, f32[25,8,128]{2,1,0:T(8,128)S(1)}, u32[]{:S(2)}, u32[]{:S(2)}) %collective-permute-start.9) | collective-permute-done | bytes 102432 | tf_op jit(solution)/shard_map/ppermute | solution.py:161
  22.0 0.0 collective-permute-done.1.refs_1_
  22.0 0.0 collective-permute-done.2.refs_3_
  22.0 3.3 %solve.1 = f32[24,128]{1,0:T(8,128)} custom-call(f32[512,128]{1,0:T(8,128)S(1)} %copy-done, f32[512,128]{1,0:T(8,128)S(1)} %collective-permute-done.1.refs_1_, f32[512,128]{1,0:T(8,128)S(1)} %collective-permute-done.refs_2_, f32[512,128]{1,0:T(8,128)S(1)} %collective-permute-done.2.refs_3_, f32[128,128]{1,0:T(8,128)S(1)} %add_add_fusion.refs_4_, ...), custom_call_target="tpu_custom_call" | custom-call | tf_op jit(solution)/shard_map/solve/pallas_call | solution.py:207
  (5 shorter events, 0.1 us)
Async XLA Ops:
  0.0 15.2 %collective-permute-start = (f32[512,128]{1,0:T(8,128)}, f32[512,128]{1,0:T(8,128)S(1)}, u32[]{:S(2)}, u32[]{:S(2)}) collective-permute-start(f32[512,128]{1,0:T(8,128)} %refs_0_.3), channel_id=1, source_target_pairs={{0,8},{4,12},{8,16},{12,20},{16,24},{20,28},{24,0},{28,4},{1,9},{5... | collective-permute-start | bytes 786440 | tf_op jit(solution)/shard_map/ppermute | solution.py:165
  4.2 4.7 %collective-permute-start.3 = (f32[25,8,128]{2,1,0:T(8,128)S(1)}, f32[25,8,128]{2,1,0:T(8,128)S(1)}, u32[]{:S(2)}, u32[]{:S(2)}) collective-permute-start(f32[25,8,128]{2,1,0:T(8,128)S(1)} %get-tuple-element.14), channel_id=1, source_target_pairs={{0,1},{1,0},{2,3},{3,2},{4,5},{5,4},{6,7},{7,6},{8,9},{9,8},{10,11... | collective-permute-start | bytes 307208 | tf_op jit(solution)/shard_map/ppermute | solution.py:161
  5.9 0.9 %copy-start = (f32[512,128]{1,0:T(8,128)S(1)}, f32[512,128]{1,0:T(8,128)}, u32[]{:S(2)}) copy-start(f32[512,128]{1,0:T(8,128)} %refs_0_.3) | copy-start | bytes 786436
  7.2 1.3 %collective-permute-start.4 = (f32[128,128]{1,0:T(8,128)S(1)}, f32[128,128]{1,0:T(8,128)S(1)}, u32[]{:S(2)}, u32[]{:S(2)}) collective-permute-start(f32[128,128]{1,0:T(8,128)S(1)} %gram.1), channel_id=1, source_target_pairs={{0,4},{4,0},{8,12},{12,8},{16,20},{20,16},{24,28},{28,24},{1,5},{5... | collective-permute-start | bytes 196616 | tf_op jit(solution)/shard_map/ppermute | solution.py:161
  9.0 7.7 %collective-permute-start.8 = (f32[25,8,128]{2,1,0:T(8,128)S(1)}, f32[25,8,128]{2,1,0:T(8,128)S(1)}, u32[]{:S(2)}, u32[]{:S(2)}) collective-permute-start(f32[25,8,128]{2,1,0:T(8,128)S(1)} %add.18), channel_id=1, source_target_pairs={{0,2},{1,3},{2,0},{3,1},{4,6},{5,7},{6,4},{7,5},{8,10},{9,11},{10,... | collective-permute-start | bytes 307208 | tf_op jit(solution)/shard_map/ppermute | solution.py:165
  11.6 5.0 %collective-permute-start.7 = (f32[128,128]{1,0:T(8,128)S(1)}, f32[128,128]{1,0:T(8,128)S(1)}, u32[]{:S(2)}, u32[]{:S(2)}) collective-permute-start(f32[128,128]{1,0:T(8,128)S(1)} %add.19), channel_id=1, source_target_pairs={{0,24},{4,28},{8,0},{12,4},{16,8},{20,12},{24,16},{28,20},{1,25},{... | collective-permute-start | bytes 196616 | tf_op jit(solution)/shard_map/ppermute | solution.py:165
  13.1 5.0 %collective-permute-start.6 = (f32[128,128]{1,0:T(8,128)S(1)}, f32[128,128]{1,0:T(8,128)S(1)}, u32[]{:S(2)}, u32[]{:S(2)}) collective-permute-start(f32[128,128]{1,0:T(8,128)S(1)} %add.19), channel_id=1, source_target_pairs={{0,16},{4,20},{8,24},{12,28},{16,0},{20,4},{24,8},{28,12},{1,17},{... | collective-permute-start | bytes 196616 | tf_op jit(solution)/shard_map/ppermute | solution.py:165
  14.6 5.3 %collective-permute-start.5 = (f32[128,128]{1,0:T(8,128)S(1)}, f32[128,128]{1,0:T(8,128)S(1)}, u32[]{:S(2)}, u32[]{:S(2)}) collective-permute-start(f32[128,128]{1,0:T(8,128)S(1)} %add.19), channel_id=1, source_target_pairs={{0,8},{4,12},{8,16},{12,20},{16,24},{20,28},{24,0},{28,4},{1,9},{5... | collective-permute-start | bytes 196616 | tf_op jit(solution)/shard_map/ppermute | solution.py:165
  15.2 6.9 %collective-permute-start.1 = (f32[512,128]{1,0:T(8,128)S(1)}, f32[512,128]{1,0:T(8,128)S(1)}, u32[]{:S(2)}, u32[]{:S(2)}) collective-permute-start(f32[512,128]{1,0:T(8,128)S(1)} %copy-done), channel_id=1, source_target_pairs={{0,4},{4,16},{8,12},{12,24},{16,20},{20,0},{24,28},{28,8},{1,5},{5... | collective-permute-start | bytes 786440 | tf_op jit(solution)/shard_map/ppermute | solution.py:185
  16.6 5.4 %collective-permute-start.2 = (f32[512,128]{1,0:T(8,128)S(1)}, f32[512,128]{1,0:T(8,128)S(1)}, u32[]{:S(2)}, u32[]{:S(2)}) collective-permute-start(f32[512,128]{1,0:T(8,128)S(1)} %collective-permute-done.refs_2_), channel_id=1, source_target_pairs={{0,4},{4,0},{8,12},{12,8},{16,20},{20,16},{24,28},{28,24},{1,5},{5... | collective-permute-start | bytes 786440 | tf_op jit(solution)/shard_map/ppermute | solution.py:161
  16.7 5.4 %collective-permute-start.9 = (f32[25,8,128]{2,1,0:T(8,128)S(1)}, f32[25,8,128]{2,1,0:T(8,128)S(1)}, u32[]{:S(2)}, u32[]{:S(2)}) collective-permute-start(f32[25,8,128]{2,1,0:T(8,128)S(1)} %add.23.refs_5_), channel_id=1, source_target_pairs={{0,1},{1,0},{2,3},{3,2},{4,5},{5,4},{6,7},{7,6},{8,9},{9,8},{10,11... | collective-permute-start | bytes 307208 | tf_op jit(solution)/shard_map/ppermute | solution.py:161

commit v3 on v2

--- a/solution.py
+++ b/solution.py
@@ -51,11 +51,15 @@
     send[...] = acc[pl.ds((1 - upper) * half, half)]
 
 
-def gram_kernel(emb, out):
-    value = emb[...]
-    out[...] = lax.dot_general(
-        value, value, (((0,), (0,)), ((), ())), precision=lax.Precision.HIGHEST, preferred_element_type=jnp.float32
-    )
+def gram_kernel(emb, second, out):
+    total = 0.0
+    for shard in (emb, second):
+        high, low = split_parts(shard[...])
+        upright = jnp.concatenate([high, low], axis=1).astype(jnp.bfloat16)
+        across = jnp.concatenate([high.T, low.T], axis=0).astype(jnp.bfloat16)
+        total = total + jnp.dot(across, upright, preferred_element_type=jnp.float32)
+    total = total[:LANES] + total[LANES:]
+    out[...] = total[:, :LANES] + total[:, LANES:]
 
 
 def solve_kernel(item_blocks, half, *refs):
@@ -181,27 +185,27 @@
     )(*[pltpu.with_memory_space_constraint(a, pltpu.HBM) for a in (*slot_arrays, confidences)])
     keep = keep + pair(send, "split")
 
-    second, sent = lax.optimization_barrier((shifted(item_emb, "item", 2), item_emb))
+    second = shifted(item_emb, "item", 2)
+    keep, sent = lax.optimization_barrier((keep, item_emb))
     first = lax.ppermute(sent, "item", [(i, (i + (3 if i % 2 else 1)) % n_item) for i in range(n_item)])
-    third = pair(second, "item")
-
-    gram = pl.pallas_call(
+    total = keep
+    for steps in range(2, n_split, 2):
+        total = total + shifted(keep, "split", steps)
+    ready, _ = lax.optimization_barrier((second, keep))
+    two_gram = pl.pallas_call(
         gram_kernel,
         out_shape=jax.ShapeDtypeStruct((features, features), f32),
-        in_specs=[vmem],
+        in_specs=[vmem] * 2,
         out_specs=vmem,
         compiler_params=params,
         name="gram",
-    )(item_emb)
-    chip_gram = gram + pair(gram, "item")
-    keep, chip_gram = lax.optimization_barrier((keep, chip_gram))
-    gram = chip_gram
-    for steps in range(2, n_item, 2):
-        gram = gram + shifted(chip_gram, "item", steps)
-
-    total = keep
-    for steps in range(2, n_split, 2):
-        total = total + shifted(keep, "split", steps)
+    )(item_emb, ready)
+    four_gram = two_gram + pair(two_gram, "item")
+    total, four_gram, ready = lax.optimization_barrier((total, four_gram, ready))
+    third = pair(ready, "item")
+    gram = four_gram
+    for steps in range(STEPS, n_item, STEPS):
+        gram = gram + shifted(four_gram, "item", steps)
     other = pair(total, "split")
 
     return pl.pallas_call(

time: 25.5 us -> 24.3 us (0.953)
  starting transfers between devices: 12.2 us -> 11.2 us
  local copies, waits for them, and re-layouts: 0.95 us -> 0.01 us
  waiting for transfers between devices: 7.12 us -> 7.85 us
    ppermute x5 -> x3, starting transfers between devices: 9.13 us -> 7.11 us  [shifted(): lax.ppermute(value, axis, [(i, (i + steps) % count) for i in range(count)])]
    ppermute x5 -> x3, waiting for transfers between devices: 3.36 us -> 4.75 us  [shifted(): lax.ppermute(value, axis, [(i, (i + steps) % count) for i in range(count)])]
    unnamed x2, local copies, waits for them, and re-layouts: 0.95 us -> 0.01 us
    ppermute x4, waiting for transfers between devices: 3.77 us -> 3.09 us  [pair(): lax.ppermute(value, axis, [(i, i ^ 1) for i in range(lax.axis_size(axis))])]
    ppermute x4, starting transfers between devices: 3.01 us -> 3.61 us  [pair(): lax.ppermute(value, axis, [(i, i ^ 1) for i in range(lax.axis_size(axis))])]
    ppermute x1, starting transfers between devices: 0.01 us -> 0.5 us  [body(): lax.ppermute(sent, 'item', [(i, (i + (3 if i % 2 else 1)) % n_item) for i...]
  transfers between devices with their start and end apart: 10 -> 8, of which waited for: 6 -> 3; matrix products, arithmetic and copies ran while one was open for 0% -> 0% of each run, Pallas kernels for 7% -> 7%
where the time goes in v3:
time: 24.3 us; the launch traced here: 24.2 us
  starting transfers between devices  11.2 us (46%)
  waiting for transfers between devices  7.85 us (32%)
  Pallas kernels  4.99 us (21%)
    ppermute x3, starting transfers between devices, shifted(): lax.ppermute(value, axis, [(i, (i + steps) % count) for i in range(count)])  7.11 us
    ppermute x3, waiting for transfers between devices, shifted(): lax.ppermute(value, axis, [(i, (i + steps) % count) for i in range(count)])  4.75 us
    ppermute x4, starting transfers between devices, pair(): lax.ppermute(value, axis, [(i, i ^ 1) for i in range(lax.axis_size(axis))])  3.61 us
    pallas_call x1, Pallas kernels, body(): pl.pallas_call(functools.partial(solve_kernel, item_blocks, half), out_sh...  3.31 us
    ppermute x4, waiting for transfers between devices, pair(): lax.ppermute(value, axis, [(i, i ^ 1) for i in range(lax.axis_size(axis))])  3.09 us
    pallas_call x1, Pallas kernels, body(): pl.pallas_call(functools.partial(weights_kernel, item_blocks, half), out_...  1.28 us
    ppermute x1, starting transfers between devices, body(): lax.ppermute(sent, 'item', [(i, (i + (3 if i % 2 else 1)) % n_item) for i...  0.5 us
  transfers between devices with their start and end apart: 8, of which 3 were waited for; matrix products, arithmetic and copies ran while one was open for 0% of the time, Pallas kernels for 7%

profile of v3, /device:TPU:0, one launch (start us, length us, event | category | flops | bytes accessed | tf_op | source)
XLA Modules:
  0.0 24.2 jit_solution(4964941626981586601)
XLA Ops:
  0.0 0.0 copy-start
  0.0 2.9 %collective-permute-start.2 = (f32[512,128]{1,0:T(8,128)}, f32[512,128]{1,0:T(8,128)S(1)}, u32[]{:S(2)}, u32[]{:S(2)}) collective-permute-start(f32[512,128]{1,0:T(8,128)} %refs_0_.3), channel_id=1, source_target_pairs={{0,8},{4,12},{8,16},{12,20},{16,24},{20,28},{24,0},{28,4},{1,9},{5... | collective-permute-start | bytes 786440 | tf_op jit(solution)/shard_map/ppermute | solution.py:169
  2.9 1.3 %weights.1 = (f32[25,8,128]{2,1,0:T(8,128)S(1)}, f32[25,8,128]{2,1,0:T(8,128)S(1)}) custom-call(s32[1,1,4,16]{3,2,1,0:T(4,128)} %refs_0_.2, s32[1,1,4,16]{3,2,1,0:T(4,128)} %refs_1_.1, s32[1,1,4,16]{3,2,1,0:T(4,128)} %refs_2_.1, s32[1,1,4]{2,1,0:T(1,128)} %refs_3_.1, bf16[1,1,4,16,8,128]{5,4,3,2,1,0:T(8,128)(2,1)} %refs_4_.1), custom_call_target="tpu_custom_call" | custom-call | tf_op jit(solution)/shard_map/weights/pallas_call | solution.py:172
  4.2 1.6 %collective-permute-start = (f32[25,8,128]{2,1,0:T(8,128)S(1)}, f32[25,8,128]{2,1,0:T(8,128)S(1)}, u32[]{:S(2)}, u32[]{:S(2)}) collective-permute-start(f32[25,8,128]{2,1,0:T(8,128)S(1)} %get-tuple-element.14), channel_id=1, source_target_pairs={{0,1},{1,0},{2,3},{3,2},{4,5},{5,4},{6,7},{7,6},{8,9},{9,8},{10,11... | collective-permute-start | bytes 307208 | tf_op jit(solution)/shard_map/ppermute | solution.py:165
  5.9 3.1 %collective-permute-done = f32[25,8,128]{2,1,0:T(8,128)S(1)} collective-permute-done((f32[25,8,128]{2,1,0:T(8,128)S(1)}, f32[25,8,128]{2,1,0:T(8,128)S(1)}, u32[]{:S(2)}, u32[]{:S(2)}) %collective-permute-start) | collective-permute-done | bytes 102432 | tf_op jit(solution)/shard_map/ppermute | solution.py:165
  9.0 2.7 %collective-permute-start.3 = (f32[25,8,128]{2,1,0:T(8,128)S(1)}, f32[25,8,128]{2,1,0:T(8,128)S(1)}, u32[]{:S(2)}, u32[]{:S(2)}) collective-permute-start(f32[25,8,128]{2,1,0:T(8,128)S(1)} %add.12), channel_id=1, source_target_pairs={{0,2},{1,3},{2,0},{3,1},{4,6},{5,7},{6,4},{7,5},{8,10},{9,11},{10,... | collective-permute-start | bytes 307208 | tf_op jit(solution)/shard_map/ppermute | solution.py:169
  11.6 0.0 collective-permute-done.2.second.refs_2_
  11.6 0.0 copy-done
  11.6 0.4 %gram.1 = f32[128,128]{1,0:T(8,128)S(1)} custom-call(f32[512,128]{1,0:T(8,128)S(1)} %copy-done, f32[512,128]{1,0:T(8,128)S(1)} %collective-permute-done.2.second.refs_2_), custom_call_target="tpu_custom_call" | custom-call | tf_op jit(solution)/shard_map/gram/pallas_call | solution.py:195
  12.0 0.1 collective-permute-start.4
  12.1 0.5 %collective-permute-start.1 = (f32[512,128]{1,0:T(8,128)S(1)}, f32[512,128]{1,0:T(8,128)S(1)}, u32[]{:S(2)}, u32[]{:S(2)}) collective-permute-start(f32[512,128]{1,0:T(8,128)S(1)} %copy-done), channel_id=1, source_target_pairs={{0,4},{4,16},{8,12},{12,24},{16,20},{20,0},{24,28},{28,8},{1,5},{5... | collective-permute-start | bytes 786440 | tf_op jit(solution)/shard_map/ppermute | solution.py:190
  12.6 2.0 %collective-permute-done.3 = f32[25,8,128]{2,1,0:T(8,128)S(1)} collective-permute-done((f32[25,8,128]{2,1,0:T(8,128)S(1)}, f32[25,8,128]{2,1,0:T(8,128)S(1)}, u32[]{:S(2)}, u32[]{:S(2)}) %collective-permute-start.3) | collective-permute-done | bytes 102432 | tf_op jit(solution)/shard_map/ppermute | solution.py:169
  14.6 0.0 collective-permute-done.4
  14.7 0.1 collective-permute-start.5
  14.7 1.8 %collective-permute-start.7 = (f32[25,8,128]{2,1,0:T(8,128)S(1)}, f32[25,8,128]{2,1,0:T(8,128)S(1)}, u32[]{:S(2)}, u32[]{:S(2)}) collective-permute-start(f32[25,8,128]{2,1,0:T(8,128)S(1)} %add.13.refs_5_), channel_id=1, source_target_pairs={{0,1},{1,0},{2,3},{3,2},{4,5},{5,4},{6,7},{7,6},{8,9},{9,8},{10,11... | collective-permute-start | bytes 307208 | tf_op jit(solution)/shard_map/ppermute | solution.py:165
  16.6 1.5 %collective-permute-start.6 = (f32[128,128]{1,0:T(8,128)S(1)}, f32[128,128]{1,0:T(8,128)S(1)}, u32[]{:S(2)}, u32[]{:S(2)}) collective-permute-start(f32[128,128]{1,0:T(8,128)S(1)} %add.14), channel_id=1, source_target_pairs={{0,16},{4,20},{8,24},{12,28},{16,0},{20,4},{24,8},{28,12},{1,17},{... | collective-permute-start | bytes 196616 | tf_op jit(solution)/shard_map/ppermute | solution.py:169
  18.1 2.8 %collective-permute-done.6 = f32[128,128]{1,0:T(8,128)S(1)} collective-permute-done((f32[128,128]{1,0:T(8,128)S(1)}, f32[128,128]{1,0:T(8,128)S(1)}, u32[]{:S(2)}, u32[]{:S(2)}) %collective-permute-start.6) | collective-permute-done | bytes 65568 | tf_op jit(solution)/shard_map/ppermute | solution.py:169
  20.8 0.0 collective-permute-done.1.refs_1_
  20.9 0.0 collective-permute-done.7.refs_6_
  20.9 0.0 collective-permute-done.5.refs_3_
  20.9 3.3 %solve.1 = f32[24,128]{1,0:T(8,128)} custom-call(f32[512,128]{1,0:T(8,128)S(1)} %copy-done, f32[512,128]{1,0:T(8,128)S(1)} %collective-permute-done.1.refs_1_, f32[512,128]{1,0:T(8,128)S(1)} %collective-permute-done.2.second.refs_2_, f32[512,128]{1,0:T(8,128)S(1)} %collective-permute-done.5.refs_3_, f32[128,128]{1,0:T(8,128)S(1)} %add.15.refs_4_, ...), custom_call_target="tpu_custom_call" | custom-call | tf_op jit(solution)/shard_map/solve/pallas_call | solution.py:211
  (4 shorter events, 0.1 us)
Async XLA Ops:
  0.0 11.6 %copy-start = (f32[512,128]{1,0:T(8,128)S(1)}, f32[512,128]{1,0:T(8,128)}, u32[]{:S(2)}) copy-start(f32[512,128]{1,0:T(8,128)} %refs_0_.3) | copy-start | bytes 786436
  0.0 11.6 %collective-permute-start.2 = (f32[512,128]{1,0:T(8,128)}, f32[512,128]{1,0:T(8,128)S(1)}, u32[]{:S(2)}, u32[]{:S(2)}) collective-permute-start(f32[512,128]{1,0:T(8,128)} %refs_0_.3), channel_id=1, source_target_pairs={{0,8},{4,12},{8,16},{12,20},{16,24},{20,28},{24,0},{28,4},{1,9},{5... | collective-permute-start | bytes 786440 | tf_op jit(solution)/shard_map/ppermute | solution.py:169
  4.2 4.7 %collective-permute-start = (f32[25,8,128]{2,1,0:T(8,128)S(1)}, f32[25,8,128]{2,1,0:T(8,128)S(1)}, u32[]{:S(2)}, u32[]{:S(2)}) collective-permute-start(f32[25,8,128]{2,1,0:T(8,128)S(1)} %get-tuple-element.14), channel_id=1, source_target_pairs={{0,1},{1,0},{2,3},{3,2},{4,5},{5,4},{6,7},{7,6},{8,9},{9,8},{10,11... | collective-permute-start | bytes 307208 | tf_op jit(solution)/shard_map/ppermute | solution.py:165
  9.0 5.6 %collective-permute-start.3 = (f32[25,8,128]{2,1,0:T(8,128)S(1)}, f32[25,8,128]{2,1,0:T(8,128)S(1)}, u32[]{:S(2)}, u32[]{:S(2)}) collective-permute-start(f32[25,8,128]{2,1,0:T(8,128)S(1)} %add.12), channel_id=1, source_target_pairs={{0,2},{1,3},{2,0},{3,1},{4,6},{5,7},{6,4},{7,5},{8,10},{9,11},{10,... | collective-permute-start | bytes 307208 | tf_op jit(solution)/shard_map/ppermute | solution.py:169
  12.0 2.6 %collective-permute-start.4 = (f32[128,128]{1,0:T(8,128)S(1)}, f32[128,128]{1,0:T(8,128)S(1)}, u32[]{:S(2)}, u32[]{:S(2)}) collective-permute-start(f32[128,128]{1,0:T(8,128)S(1)} %gram.1), channel_id=1, source_target_pairs={{0,4},{4,0},{8,12},{12,8},{16,20},{20,16},{24,28},{28,24},{1,5},{5... | collective-permute-start | bytes 196616 | tf_op jit(solution)/shard_map/ppermute | solution.py:165
  12.1 8.7 %collective-permute-start.1 = (f32[512,128]{1,0:T(8,128)S(1)}, f32[512,128]{1,0:T(8,128)S(1)}, u32[]{:S(2)}, u32[]{:S(2)}) collective-permute-start(f32[512,128]{1,0:T(8,128)S(1)} %copy-done), channel_id=1, source_target_pairs={{0,4},{4,16},{8,12},{12,24},{16,20},{20,0},{24,28},{28,8},{1,5},{5... | collective-permute-start | bytes 786440 | tf_op jit(solution)/shard_map/ppermute | solution.py:190
  14.7 6.2 %collective-permute-start.5 = (f32[512,128]{1,0:T(8,128)S(1)}, f32[512,128]{1,0:T(8,128)S(1)}, u32[]{:S(2)}, u32[]{:S(2)}) collective-permute-start(f32[512,128]{1,0:T(8,128)S(1)} %collective-permute-done.2.second.refs_2_), channel_id=1, source_target_pairs={{0,4},{4,0},{8,12},{12,8},{16,20},{20,16},{24,28},{28,24},{1,5},{5... | collective-permute-start | bytes 786440 | tf_op jit(solution)/shard_map/ppermute | solution.py:165
  14.7 6.1 %collective-permute-start.7 = (f32[25,8,128]{2,1,0:T(8,128)S(1)}, f32[25,8,128]{2,1,0:T(8,128)S(1)}, u32[]{:S(2)}, u32[]{:S(2)}) collective-permute-start(f32[25,8,128]{2,1,0:T(8,128)S(1)} %add.13.refs_5_), channel_id=1, source_target_pairs={{0,1},{1,0},{2,3},{3,2},{4,5},{5,4},{6,7},{7,6},{8,9},{9,8},{10,11... | collective-permute-start | bytes 307208 | tf_op jit(solution)/shard_map/ppermute | solution.py:165
  16.6 4.3 %collective-permute-start.6 = (f32[128,128]{1,0:T(8,128)S(1)}, f32[128,128]{1,0:T(8,128)S(1)}, u32[]{:S(2)}, u32[]{:S(2)}) collective-permute-start(f32[128,128]{1,0:T(8,128)S(1)} %add.14), channel_id=1, source_target_pairs={{0,16},{4,20},{8,24},{12,28},{16,0},{20,4},{24,8},{28,12},{1,17},{... | collective-permute-start | bytes 196616 | tf_op jit(solution)/shard_map/ppermute | solution.py:169

commit v4 on v3

--- a/solution.py
+++ b/solution.py
@@ -11,6 +11,9 @@
 STEPS = 4
 CG_ITERS = 3
 RIDGE = 0.1
+SUM_COST = 400000000
+BASE_COST = 1800000000
+GRAM_COST = 0
 VMEM_LIMIT = 16 * 2**20
 
 SUB = 8
@@ -62,9 +65,20 @@
     out[...] = total[:, :LANES] + total[:, LANES:]
 
 
+def sum_kernel(*refs):
+    refs[-1][...] = functools.reduce(jnp.add, [ref[...] for ref in refs[:-1]])
+
+
+def base_kernel(gram, out):
+    rows = lax.broadcasted_iota(jnp.int32, gram.shape, 0)
+    columns = lax.broadcasted_iota(jnp.int32, gram.shape, 1)
+    high, low = split_parts(gram[...] + jnp.where(rows == columns, RIDGE, 0.0))
+    out[...] = jnp.concatenate([high, low], axis=1).astype(jnp.bfloat16)
+
+
 def solve_kernel(item_blocks, half, *refs):
     shards = refs[:STEPS]
-    gram, keep, other, out, weights, wide, tall = refs[STEPS:]
+    base_pair, keep, other, out, weights, wide, tall = refs[STEPS:]
     cells = STEPS * item_blocks
     upper = lax.rem(lax.axis_index("split"), 2)
     users = USER_BLOCKS * SUB
@@ -77,12 +91,6 @@
         high, low = split_parts(shards[k][...])
         tall[k] = jnp.concatenate([high, low], axis=1).astype(jnp.bfloat16)
         wide[k] = jnp.concatenate([high.T, low.T], axis=0).astype(jnp.bfloat16)
-
-    eye_rows = lax.broadcasted_iota(jnp.int32, (features, features), 0)
-    eye_cols = lax.broadcasted_iota(jnp.int32, (features, features), 1)
-    base = gram[...] + jnp.where(eye_rows == eye_cols, RIDGE, 0.0)
-    base_high, base_low = split_parts(base)
-    base_pair = jnp.concatenate([base_high, base_low], axis=1).astype(jnp.bfloat16)
 
     def conf_of(k):
         return jnp.concatenate(
@@ -122,29 +130,46 @@
 
     right = folded(sum(back(conf_of(k) + count_of(k), k) for k in range(STEPS)))
 
-    def apply(direction):
-        high, low = split_parts(direction)
+    def scores_of(value):
+        high, low = split_parts(value)
         left = jnp.concatenate(
             [jnp.concatenate([high, high], axis=1), jnp.concatenate([low, low], axis=1)], axis=0
         ).astype(jnp.bfloat16)
-        total = jnp.dot(left[:, :features], base_pair, preferred_element_type=jnp.float32)
+        through = folded(jnp.dot(left[:, :features], base_pair[...], preferred_element_type=jnp.float32))
+        scores = []
         for k in range(STEPS):
-            scores = jnp.dot(left, wide[k], preferred_element_type=jnp.float32)
-            total = total + back((scores[:users] + scores[users:]) * conf_of(k), k)
-        return folded(total)
-
+            both = jnp.dot(left, wide[k], preferred_element_type=jnp.float32)
+            scores.append(both[:users] + both[users:])
+        return [through] + scores
+
+    def curvature(direction, products, weighted):
+        curve = direction * products[0]
+        for k in range(STEPS):
+            terms = weighted[k] * products[1 + k]
+            for i in range(item_blocks):
+                curve = curve + terms[:, i * LANES : (i + 1) * LANES]
+        return jnp.sum(curve, axis=1, keepdims=True)
+
+    confs = [conf_of(k) for k in range(STEPS)]
     answer = jnp.zeros_like(right)
     residual = right
     direction = right
     norm_now = jnp.sum(residual * residual, axis=1, keepdims=True)
+    residual_products = scores_of(residual)
+    products = residual_products
     for iteration in range(CG_ITERS):
-        image = apply(direction)
-        step = norm_now / jnp.sum(direction * image, axis=1, keepdims=True)
+        weighted = [products[1 + k] * confs[k] for k in range(STEPS)]
+        step = norm_now / curvature(direction, products, weighted)
         answer = answer + step * direction
         if iteration + 1 < CG_ITERS:
+            image = products[0] + folded(sum(back(weighted[k], k) for k in range(STEPS)))
+            image_products = scores_of(image)
             residual = residual - step * image
             norm_next = jnp.sum(residual * residual, axis=1, keepdims=True)
-            direction = residual + (norm_next / norm_now) * direction
+            ratio = norm_next / norm_now
+            direction = residual + ratio * direction
+            residual_products = [r - step * i for r, i in zip(residual_products, image_products)]
+            products = [r + ratio * p for r, p in zip(residual_products, products)]
             norm_now = norm_next
     out[...] = answer
 
@@ -167,6 +192,9 @@
     def shifted(value, axis, steps):
         count = lax.axis_size(axis)
         return lax.ppermute(value, axis, [(i, (i + steps) % count) for i in range(count)])
+
+    def cost(flops):
+        return pl.CostEstimate(flops=flops, bytes_accessed=0, transcendentals=0)
 
     slot_arrays = (user_block, item_block, block_age, block_count)
     keep, send = pl.pallas_call(
@@ -183,14 +211,19 @@
         compiler_params=params,
         name="weights",
     )(*[pltpu.with_memory_space_constraint(a, pltpu.HBM) for a in (*slot_arrays, confidences)])
-    keep = keep + pair(send, "split")
-
-    second = shifted(item_emb, "item", 2)
-    keep, sent = lax.optimization_barrier((keep, item_emb))
-    first = lax.ppermute(sent, "item", [(i, (i + (3 if i % 2 else 1)) % n_item) for i in range(n_item)])
+    sent = item_emb
+    with jax.named_scope("near_halves"):
+        keep = keep + pair(send, "split")
+
+    with jax.named_scope("second_shard"):
+        second = shifted(sent, "item", 2)
+    sent = item_emb
+    with jax.named_scope("first_shard"):
+        first = lax.ppermute(sent, "item", [(i, (i + (3 if i % 2 else 1)) % n_item) for i in range(n_item)])
     total = keep
-    for steps in range(2, n_split, 2):
-        total = total + shifted(keep, "split", steps)
+    with jax.named_scope("far_halves"):
+        for steps in range(2, n_split, 2):
+            total = total + shifted(keep, "split", steps)
     ready, _ = lax.optimization_barrier((second, keep))
     two_gram = pl.pallas_call(
         gram_kernel,
@@ -198,15 +231,37 @@
         in_specs=[vmem] * 2,
         out_specs=vmem,
         compiler_params=params,
+        cost_estimate=cost(GRAM_COST),
         name="gram",
     )(item_emb, ready)
-    four_gram = two_gram + pair(two_gram, "item")
-    total, four_gram, ready = lax.optimization_barrier((total, four_gram, ready))
-    third = pair(ready, "item")
-    gram = four_gram
-    for steps in range(STEPS, n_item, STEPS):
-        gram = gram + shifted(four_gram, "item", steps)
-    other = pair(total, "split")
+    with jax.named_scope("chip_gram"):
+        four_gram = two_gram + pair(two_gram, "item")
+    with jax.named_scope("all_gram"):
+        grams = [shifted(four_gram, "item", steps) for steps in range(STEPS, n_item, STEPS)]
+    gram = pl.pallas_call(
+        sum_kernel,
+        out_shape=jax.ShapeDtypeStruct((features, features), f32),
+        in_specs=[vmem] * (1 + len(grams)),
+        out_specs=vmem,
+        compiler_params=params,
+        cost_estimate=cost(SUM_COST),
+        name="sum",
+    )(four_gram, *grams)
+    total, ready = lax.optimization_barrier((total, ready))
+    with jax.named_scope("third_shard"):
+        third = pair(ready, "item")
+    gram, first = lax.optimization_barrier((gram, first))
+    base_pair = pl.pallas_call(
+        base_kernel,
+        out_shape=jax.ShapeDtypeStruct((features, 2 * features), jnp.bfloat16),
+        in_specs=[vmem],
+        out_specs=vmem,
+        compiler_params=params,
+        cost_estimate=cost(BASE_COST),
+        name="base",
+    )(gram)
+    with jax.named_scope("other_half"):
+        other = pair(total, "split")
 
     return pl.pallas_call(
         functools.partial(solve_kernel, item_blocks, half),
@@ -220,7 +275,7 @@
         ],
         compiler_params=params,
         name="solve",
-    )(item_emb, first, second, third, gram, total, other)
+    )(item_emb, first, second, third, base_pair, total, other)
 
 
 def solution(mesh):

time: 24.3 us -> 23.3 us (0.959)
  starting transfers between devices: 11.2 us -> 10.6 us
  Pallas kernels: 4.99 us -> 4.47 us
    ppermute x4, waiting for transfers between devices: 3.09 us -> 6.92 us  [pair(): lax.ppermute(value, axis, [(i, i ^ 1) for i in range(lax.axis_size(axis))])]
    ppermute x3, waiting for transfers between devices: 4.75 us -> 1.01 us  [shifted(): lax.ppermute(value, axis, [(i, (i + steps) % count) for i in range(count)])]
    pallas_call x1, Pallas kernels: 3.31 us -> 2.77 us  [body(): pl.pallas_call(functools.partial(solve_kernel, item_blocks, half), out_sh...]
    ppermute x1, starting transfers between devices: 0.5 us -> 0.01 us  [body(): lax.ppermute(sent, 'item', [(i, (i + (3 if i % 2 else 1)) % n_item) for i...]
  transfers between devices with their start and end apart: 8 -> 8, of which waited for: 3 -> 4; matrix products, arithmetic and copies ran while one was open for 0% -> 0% of each run, Pallas kernels for 7% -> 7%
where the time goes in v4:
time: 23.3 us; the launch traced here: 23.1 us
  starting transfers between devices  10.6 us (45%)
  waiting for transfers between devices  7.94 us (34%)
  Pallas kernels  4.47 us (19%)
    ppermute x3, starting transfers between devices, shifted(): lax.ppermute(value, axis, [(i, (i + steps) % count) for i in range(count)])  7.19 us
    ppermute x4, waiting for transfers between devices, pair(): lax.ppermute(value, axis, [(i, i ^ 1) for i in range(lax.axis_size(axis))])  6.92 us
    ppermute x4, starting transfers between devices, pair(): lax.ppermute(value, axis, [(i, i ^ 1) for i in range(lax.axis_size(axis))])  3.43 us
    pallas_call x1, Pallas kernels, body(): pl.pallas_call(functools.partial(solve_kernel, item_blocks, half), out_sh...  2.77 us
    pallas_call x1, Pallas kernels, body(): pl.pallas_call(functools.partial(weights_kernel, item_blocks, half), out_...  1.28 us
    ppermute x3, waiting for transfers between devices, shifted(): lax.ppermute(value, axis, [(i, (i + steps) % count) for i in range(count)])  1.01 us
  transfers between devices with their start and end apart: 8, of which 4 were waited for; matrix products, arithmetic and copies ran while one was open for 0% of the time, Pallas kernels for 7%

profile of v4, /device:TPU:0, one launch (start us, length us, event | category | flops | bytes accessed | tf_op | source)
XLA Modules:
  0.0 23.1 jit_solution(17011960437877308188)
XLA Ops:
  0.0 0.0 copy-start
  0.0 2.9 %collective-permute-start = (f32[512,128]{1,0:T(8,128)}, f32[512,128]{1,0:T(8,128)S(1)}, u32[]{:S(2)}, u32[]{:S(2)}) collective-permute-start(f32[512,128]{1,0:T(8,128)} %refs_0_.3), channel_id=1, source_target_pairs={{0,8},{4,12},{8,16},{12,20},{16,24},{20,28},{24,0},{28,4},{1,9},{5... | collective-permute-start | bytes 786440 | tf_op jit(solution)/shard_map/second_shard/ppermute | solution.py:194
  2.9 1.3 %weights.1 = (f32[25,8,128]{2,1,0:T(8,128)S(1)}, f32[25,8,128]{2,1,0:T(8,128)S(1)}) custom-call(s32[1,1,4,16]{3,2,1,0:T(4,128)} %refs_0_.2, s32[1,1,4,16]{3,2,1,0:T(4,128)} %refs_1_.1, s32[1,1,4,16]{3,2,1,0:T(4,128)} %refs_2_.1, s32[1,1,4]{2,1,0:T(1,128)} %refs_3_.1, bf16[1,1,4,16,8,128]{5,4,3,2,1,0:T(8,128)(2,1)} %refs_4_.1), custom_call_target="tpu_custom_call" | custom-call | tf_op jit(solution)/shard_map/weights/pallas_call | solution.py:200
  4.2 1.6 %collective-permute-start.1 = (f32[25,8,128]{2,1,0:T(8,128)S(1)}, f32[25,8,128]{2,1,0:T(8,128)S(1)}, u32[]{:S(2)}, u32[]{:S(2)}) collective-permute-start(f32[25,8,128]{2,1,0:T(8,128)S(1)} %get-tuple-element.13), channel_id=1, source_target_pairs={{0,1},{1,0},{2,3},{3,2},{4,5},{5,4},{6,7},{7,6},{8,9},{9,8},{10,11... | collective-permute-start | bytes 307208 | tf_op jit(solution)/shard_map/near_halves/ppermute | solution.py:190
  5.9 0.0 collective-permute-start.4
  5.9 3.1 %collective-permute-done.1 = f32[25,8,128]{2,1,0:T(8,128)S(1)} collective-permute-done((f32[25,8,128]{2,1,0:T(8,128)S(1)}, f32[25,8,128]{2,1,0:T(8,128)S(1)}, u32[]{:S(2)}, u32[]{:S(2)}) %collective-permute-start.1) | collective-permute-done | bytes 102432 | tf_op jit(solution)/shard_map/near_halves/ppermute | solution.py:190
  9.0 2.7 %collective-permute-start.5 = (f32[25,8,128]{2,1,0:T(8,128)S(1)}, f32[25,8,128]{2,1,0:T(8,128)S(1)}, u32[]{:S(2)}, u32[]{:S(2)}) collective-permute-start(f32[25,8,128]{2,1,0:T(8,128)S(1)} %add.9), channel_id=1, source_target_pairs={{0,2},{1,3},{2,0},{3,1},{4,6},{5,7},{6,4},{7,5},{8,10},{9,11},{10,... | collective-permute-start | bytes 307208 | tf_op jit(solution)/shard_map/far_halves/ppermute | solution.py:194
  11.6 0.0 collective-permute-done.second.refs_2_
  11.6 0.0 copy-done
  11.6 0.4 %gram.1 = f32[128,128]{1,0:T(8,128)S(1)} custom-call(f32[512,128]{1,0:T(8,128)S(1)} %copy-done, f32[512,128]{1,0:T(8,128)S(1)} %collective-permute-done.second.refs_2_), custom_call_target="tpu_custom_call" | custom-call | tf_op jit(solution)/shard_map/gram/pallas_call | solution.py:228
  12.0 0.1 collective-permute-start.2
  12.1 1.2 %collective-permute-done.2 = f32[128,128]{1,0:T(8,128)S(1)} collective-permute-done((f32[128,128]{1,0:T(8,128)S(1)}, f32[128,128]{1,0:T(8,128)S(1)}, u32[]{:S(2)}, u32[]{:S(2)}) %collective-permute-start.2) | collective-permute-done | bytes 65568 | tf_op jit(solution)/shard_map/chip_gram/ppermute | solution.py:190
  13.4 1.6 %collective-permute-start.3 = (f32[128,128]{1,0:T(8,128)S(1)}, f32[128,128]{1,0:T(8,128)S(1)}, u32[]{:S(2)}, u32[]{:S(2)}) collective-permute-start(f32[128,128]{1,0:T(8,128)S(1)} %add.10.refs_0_), channel_id=1, source_target_pairs={{0,16},{4,20},{8,24},{12,28},{16,0},{20,4},{24,8},{28,12},{1,17},{... | collective-permute-start | bytes 196616 | tf_op jit(solution)/shard_map/all_gram/ppermute | solution.py:194
  15.0 0.0 collective-permute-done.5
  15.0 0.1 collective-permute-start.6
  15.1 1.6 %collective-permute-start.7 = (f32[25,8,128]{2,1,0:T(8,128)S(1)}, f32[25,8,128]{2,1,0:T(8,128)S(1)}, u32[]{:S(2)}, u32[]{:S(2)}) collective-permute-start(f32[25,8,128]{2,1,0:T(8,128)S(1)} %add.11.refs_5_), channel_id=1, source_target_pairs={{0,1},{1,0},{2,3},{3,2},{4,5},{5,4},{6,7},{7,6},{8,9},{9,8},{10,11... | collective-permute-start | bytes 307208 | tf_op jit(solution)/shard_map/other_half/ppermute | solution.py:190
  16.7 1.0 %collective-permute-done.3.refs_1_ = f32[128,128]{1,0:T(8,128)S(1)} collective-permute-done((f32[128,128]{1,0:T(8,128)S(1)}, f32[128,128]{1,0:T(8,128)S(1)}, u32[]{:S(2)}, u32[]{:S(2)}) %collective-permute-start.3) | collective-permute-done | bytes 65568 | tf_op jit(solution)/shard_map/all_gram/ppermute | solution.py:194
  17.7 0.0 collective-permute-done.4.refs_1_
  17.8 2.6 %collective-permute-done.7.refs_6_ = f32[25,8,128]{2,1,0:T(8,128)S(1)} collective-permute-done((f32[25,8,128]{2,1,0:T(8,128)S(1)}, f32[25,8,128]{2,1,0:T(8,128)S(1)}, u32[]{:S(2)}, u32[]{:S(2)}) %collective-permute-start.7) | collective-permute-done | bytes 102432 | tf_op jit(solution)/shard_map/other_half/ppermute | solution.py:190
  20.4 0.0 collective-permute-done.6.refs_3_
  20.4 2.8 %solve.1 = f32[24,128]{1,0:T(8,128)} custom-call(f32[512,128]{1,0:T(8,128)S(1)} %copy-done, f32[512,128]{1,0:T(8,128)S(1)} %collective-permute-done.4.refs_1_, f32[512,128]{1,0:T(8,128)S(1)} %collective-permute-done.second.refs_2_, f32[512,128]{1,0:T(8,128)S(1)} %collective-permute-done.6.refs_3_, bf16[128,256]{1,0:T(8,128)(2,1)S(1)} %base.1.refs_4_, ...), custom_call_target="tpu_custom_call" | custom-call | tf_op jit(solution)/shard_map/solve/pallas_call | solution.py:266
  (5 shorter events, 0.1 us)
Async XLA Ops:
  0.0 11.6 %copy-start = (f32[512,128]{1,0:T(8,128)S(1)}, f32[512,128]{1,0:T(8,128)}, u32[]{:S(2)}) copy-start(f32[512,128]{1,0:T(8,128)} %refs_0_.3) | copy-start | bytes 786436
  0.0 11.6 %collective-permute-start = (f32[512,128]{1,0:T(8,128)}, f32[512,128]{1,0:T(8,128)S(1)}, u32[]{:S(2)}, u32[]{:S(2)}) collective-permute-start(f32[512,128]{1,0:T(8,128)} %refs_0_.3), channel_id=1, source_target_pairs={{0,8},{4,12},{8,16},{12,20},{16,24},{20,28},{24,0},{28,4},{1,9},{5... | collective-permute-start | bytes 786440 | tf_op jit(solution)/shard_map/second_shard/ppermute | solution.py:194
  4.2 4.7 %collective-permute-start.1 = (f32[25,8,128]{2,1,0:T(8,128)S(1)}, f32[25,8,128]{2,1,0:T(8,128)S(1)}, u32[]{:S(2)}, u32[]{:S(2)}) collective-permute-start(f32[25,8,128]{2,1,0:T(8,128)S(1)} %get-tuple-element.13), channel_id=1, source_target_pairs={{0,1},{1,0},{2,3},{3,2},{4,5},{5,4},{6,7},{7,6},{8,9},{9,8},{10,11... | collective-permute-start | bytes 307208 | tf_op jit(solution)/shard_map/near_halves/ppermute | solution.py:190
  5.9 11.8 %collective-permute-start.4 = (f32[512,128]{1,0:T(8,128)}, f32[512,128]{1,0:T(8,128)S(1)}, u32[]{:S(2)}, u32[]{:S(2)}) collective-permute-start(f32[512,128]{1,0:T(8,128)} %refs_0_.3), channel_id=1, source_target_pairs={{0,4},{4,16},{8,12},{12,24},{16,20},{20,0},{24,28},{28,8},{1,5},{5... | collective-permute-start | bytes 786440 | tf_op jit(solution)/shard_map/first_shard/ppermute | solution.py:222
  9.0 6.0 %collective-permute-start.5 = (f32[25,8,128]{2,1,0:T(8,128)S(1)}, f32[25,8,128]{2,1,0:T(8,128)S(1)}, u32[]{:S(2)}, u32[]{:S(2)}) collective-permute-start(f32[25,8,128]{2,1,0:T(8,128)S(1)} %add.9), channel_id=1, source_target_pairs={{0,2},{1,3},{2,0},{3,1},{4,6},{5,7},{6,4},{7,5},{8,10},{9,11},{10,... | collective-permute-start | bytes 307208 | tf_op jit(solution)/shard_map/far_halves/ppermute | solution.py:194
  12.0 1.3 %collective-permute-start.2 = (f32[128,128]{1,0:T(8,128)S(1)}, f32[128,128]{1,0:T(8,128)S(1)}, u32[]{:S(2)}, u32[]{:S(2)}) collective-permute-start(f32[128,128]{1,0:T(8,128)S(1)} %gram.1), channel_id=1, source_target_pairs={{0,4},{4,0},{8,12},{12,8},{16,20},{20,16},{24,28},{28,24},{1,5},{5... | collective-permute-start | bytes 196616 | tf_op jit(solution)/shard_map/chip_gram/ppermute | solution.py:190
  13.4 4.3 %collective-permute-start.3 = (f32[128,128]{1,0:T(8,128)S(1)}, f32[128,128]{1,0:T(8,128)S(1)}, u32[]{:S(2)}, u32[]{:S(2)}) collective-permute-start(f32[128,128]{1,0:T(8,128)S(1)} %add.10.refs_0_), channel_id=1, source_target_pairs={{0,16},{4,20},{8,24},{12,28},{16,0},{20,4},{24,8},{28,12},{1,17},{... | collective-permute-start | bytes 196616 | tf_op jit(solution)/shard_map/all_gram/ppermute | solution.py:194
  15.0 5.4 %collective-permute-start.6 = (f32[512,128]{1,0:T(8,128)S(1)}, f32[512,128]{1,0:T(8,128)S(1)}, u32[]{:S(2)}, u32[]{:S(2)}) collective-permute-start(f32[512,128]{1,0:T(8,128)S(1)} %collective-permute-done.second.refs_2_), channel_id=1, source_target_pairs={{0,4},{4,0},{8,12},{12,8},{16,20},{20,16},{24,28},{28,24},{1,5},{5... | collective-permute-start | bytes 786440 | tf_op jit(solution)/shard_map/third_shard/ppermute | solution.py:190
  15.1 5.3 %collective-permute-start.7 = (f32[25,8,128]{2,1,0:T(8,128)S(1)}, f32[25,8,128]{2,1,0:T(8,128)S(1)}, u32[]{:S(2)}, u32[]{:S(2)}) collective-permute-start(f32[25,8,128]{2,1,0:T(8,128)S(1)} %add.11.refs_5_), channel_id=1, source_target_pairs={{0,1},{1,0},{2,3},{3,2},{4,5},{5,4},{6,7},{7,6},{8,9},{9,8},{10,11... | collective-permute-start | bytes 307208 | tf_op jit(solution)/shard_map/other_half/ppermute | solution.py:190

commit v5 on v4

--- a/solution.py
+++ b/solution.py
@@ -11,10 +11,10 @@
 STEPS = 4
 CG_ITERS = 3
 RIDGE = 0.1
-SUM_COST = 400000000
-BASE_COST = 1800000000
-GRAM_COST = 0
 VMEM_LIMIT = 16 * 2**20
+
+SUM_COST = 400_000_000
+BASE_COST = 1_800_000_000
 
 SUB = 8
 LANES = 128
@@ -130,46 +130,38 @@
 
     right = folded(sum(back(conf_of(k) + count_of(k), k) for k in range(STEPS)))
 
-    def scores_of(value):
-        high, low = split_parts(value)
+    def scores_of(direction):
+        high, low = split_parts(direction)
         left = jnp.concatenate(
             [jnp.concatenate([high, high], axis=1), jnp.concatenate([low, low], axis=1)], axis=0
         ).astype(jnp.bfloat16)
-        through = folded(jnp.dot(left[:, :features], base_pair[...], preferred_element_type=jnp.float32))
+        through = jnp.dot(left[:, :features], base_pair[...], preferred_element_type=jnp.float32)
         scores = []
         for k in range(STEPS):
             both = jnp.dot(left, wide[k], preferred_element_type=jnp.float32)
             scores.append(both[:users] + both[users:])
-        return [through] + scores
-
-    def curvature(direction, products, weighted):
-        curve = direction * products[0]
-        for k in range(STEPS):
-            terms = weighted[k] * products[1 + k]
-            for i in range(item_blocks):
-                curve = curve + terms[:, i * LANES : (i + 1) * LANES]
-        return jnp.sum(curve, axis=1, keepdims=True)
+        return folded(through), scores
 
     confs = [conf_of(k) for k in range(STEPS)]
     answer = jnp.zeros_like(right)
     residual = right
     direction = right
     norm_now = jnp.sum(residual * residual, axis=1, keepdims=True)
-    residual_products = scores_of(residual)
-    products = residual_products
     for iteration in range(CG_ITERS):
-        weighted = [products[1 + k] * confs[k] for k in range(STEPS)]
-        step = norm_now / curvature(direction, products, weighted)
+        through, scores = scores_of(direction)
+        weighted = [scores[k] * confs[k] for k in range(STEPS)]
+        curve = direction * through
+        for k in range(STEPS):
+            terms = weighted[k] * scores[k]
+            for i in range(item_blocks):
+                curve = curve + terms[:, i * LANES : (i + 1) * LANES]
+        step = norm_now / jnp.sum(curve, axis=1, keepdims=True)
         answer = answer + step * direction
         if iteration + 1 < CG_ITERS:
-            image = products[0] + folded(sum(back(weighted[k], k) for k in range(STEPS)))
-            image_products = scores_of(image)
+            image = through + folded(sum(back(weighted[k], k) for k in range(STEPS)))
             residual = residual - step * image
             norm_next = jnp.sum(residual * residual, axis=1, keepdims=True)
-            ratio = norm_next / norm_now
-            direction = residual + ratio * direction
-            residual_products = [r - step * i for r, i in zip(residual_products, image_products)]
-            products = [r + ratio * p for r, p in zip(residual_products, products)]
+            direction = residual + (norm_next / norm_now) * direction
             norm_now = norm_next
     out[...] = answer
 
@@ -211,15 +203,13 @@
         compiler_params=params,
         name="weights",
     )(*[pltpu.with_memory_space_constraint(a, pltpu.HBM) for a in (*slot_arrays, confidences)])
-    sent = item_emb
     with jax.named_scope("near_halves"):
         keep = keep + pair(send, "split")
 
     with jax.named_scope("second_shard"):
-        second = shifted(sent, "item", 2)
-    sent = item_emb
+        second = shifted(item_emb, "item", 2)
     with jax.named_scope("first_shard"):
-        first = lax.ppermute(sent, "item", [(i, (i + (3 if i % 2 else 1)) % n_item) for i in range(n_item)])
+        first = lax.ppermute(item_emb, "item", [(i, (i + (3 if i % 2 else 1)) % n_item) for i in range(n_item)])
     total = keep
     with jax.named_scope("far_halves"):
         for steps in range(2, n_split, 2):
@@ -231,7 +221,6 @@
         in_specs=[vmem] * 2,
         out_specs=vmem,
         compiler_params=params,
-        cost_estimate=cost(GRAM_COST),
         name="gram",
     )(item_emb, ready)
     with jax.named_scope("chip_gram"):

time: 23.3 us -> 23.4 us (level)
  no operation moved by 1% of the time
where the time goes in v5:
time: 23.4 us; the launch traced here: 23.3 us
  starting transfers between devices  10.6 us (45%)
  waiting for transfers between devices  7.94 us (34%)
  Pallas kernels  4.63 us (20%)
    ppermute x3, starting transfers between devices, shifted(): lax.ppermute(value, axis, [(i, (i + steps) % count) for i in range(count)])  7.17 us
    ppermute x4, waiting for transfers between devices, pair(): lax.ppermute(value, axis, [(i, i ^ 1) for i in range(lax.axis_size(axis))])  6.92 us
    ppermute x4, starting transfers between devices, pair(): lax.ppermute(value, axis, [(i, i ^ 1) for i in range(lax.axis_size(axis))])  3.42 us
    pallas_call x1, Pallas kernels, body(): pl.pallas_call(functools.partial(solve_kernel, item_blocks, half), out_sh...  2.92 us
    pallas_call x1, Pallas kernels, body(): pl.pallas_call(functools.partial(weights_kernel, item_blocks, half), out_...  1.28 us
    ppermute x3, waiting for transfers between devices, shifted(): lax.ppermute(value, axis, [(i, (i + steps) % count) for i in range(count)])  1.02 us
  transfers between devices with their start and end apart: 8, of which 4 were waited for; matrix products, arithmetic and copies ran while one was open for 0% of the time, Pallas kernels for 7%

profile of v5, /device:TPU:0, one launch (start us, length us, event | category | flops | bytes accessed | tf_op | source)
XLA Modules:
  0.0 23.3 jit_solution(14520133698489429151)
XLA Ops:
  0.0 0.0 copy-start
  0.0 2.9 %collective-permute-start = (f32[512,128]{1,0:T(8,128)}, f32[512,128]{1,0:T(8,128)S(1)}, u32[]{:S(2)}, u32[]{:S(2)}) collective-permute-start(f32[512,128]{1,0:T(8,128)} %refs_0_.3), channel_id=1, source_target_pairs={{0,8},{4,12},{8,16},{12,20},{16,24},{20,28},{24,0},{28,4},{1,9},{5... | collective-permute-start | bytes 786440 | tf_op jit(solution)/shard_map/second_shard/ppermute | solution.py:186
  2.9 1.3 %weights.1 = (f32[25,8,128]{2,1,0:T(8,128)S(1)}, f32[25,8,128]{2,1,0:T(8,128)S(1)}) custom-call(s32[1,1,4,16]{3,2,1,0:T(4,128)} %refs_0_.2, s32[1,1,4,16]{3,2,1,0:T(4,128)} %refs_1_.1, s32[1,1,4,16]{3,2,1,0:T(4,128)} %refs_2_.1, s32[1,1,4]{2,1,0:T(1,128)} %refs_3_.1, bf16[1,1,4,16,8,128]{5,4,3,2,1,0:T(8,128)(2,1)} %refs_4_.1), custom_call_target="tpu_custom_call" | custom-call | tf_op jit(solution)/shard_map/weights/pallas_call | solution.py:192
  4.2 1.6 %collective-permute-start.1 = (f32[25,8,128]{2,1,0:T(8,128)S(1)}, f32[25,8,128]{2,1,0:T(8,128)S(1)}, u32[]{:S(2)}, u32[]{:S(2)}) collective-permute-start(f32[25,8,128]{2,1,0:T(8,128)S(1)} %get-tuple-element.13), channel_id=1, source_target_pairs={{0,1},{1,0},{2,3},{3,2},{4,5},{5,4},{6,7},{7,6},{8,9},{9,8},{10,11... | collective-permute-start | bytes 307208 | tf_op jit(solution)/shard_map/near_halves/ppermute | solution.py:182
  5.9 0.0 collective-permute-start.4
  5.9 3.1 %collective-permute-done.1 = f32[25,8,128]{2,1,0:T(8,128)S(1)} collective-permute-done((f32[25,8,128]{2,1,0:T(8,128)S(1)}, f32[25,8,128]{2,1,0:T(8,128)S(1)}, u32[]{:S(2)}, u32[]{:S(2)}) %collective-permute-start.1) | collective-permute-done | bytes 102432 | tf_op jit(solution)/shard_map/near_halves/ppermute | solution.py:182
  9.0 2.7 %collective-permute-start.5 = (f32[25,8,128]{2,1,0:T(8,128)S(1)}, f32[25,8,128]{2,1,0:T(8,128)S(1)}, u32[]{:S(2)}, u32[]{:S(2)}) collective-permute-start(f32[25,8,128]{2,1,0:T(8,128)S(1)} %add.9), channel_id=1, source_target_pairs={{0,2},{1,3},{2,0},{3,1},{4,6},{5,7},{6,4},{7,5},{8,10},{9,11},{10,... | collective-permute-start | bytes 307208 | tf_op jit(solution)/shard_map/far_halves/ppermute | solution.py:186
  11.6 0.0 collective-permute-done.second.refs_2_
  11.6 0.0 copy-done
  11.6 0.4 %gram.1 = f32[128,128]{1,0:T(8,128)S(1)} custom-call(f32[512,128]{1,0:T(8,128)S(1)} %copy-done, f32[512,128]{1,0:T(8,128)S(1)} %collective-permute-done.second.refs_2_), custom_call_target="tpu_custom_call" | custom-call | tf_op jit(solution)/shard_map/gram/pallas_call | solution.py:218
  12.0 0.1 collective-permute-start.2
  12.1 1.2 %collective-permute-done.2 = f32[128,128]{1,0:T(8,128)S(1)} collective-permute-done((f32[128,128]{1,0:T(8,128)S(1)}, f32[128,128]{1,0:T(8,128)S(1)}, u32[]{:S(2)}, u32[]{:S(2)}) %collective-permute-start.2) | collective-permute-done | bytes 65568 | tf_op jit(solution)/shard_map/chip_gram/ppermute | solution.py:182
  13.4 1.6 %collective-permute-start.3 = (f32[128,128]{1,0:T(8,128)S(1)}, f32[128,128]{1,0:T(8,128)S(1)}, u32[]{:S(2)}, u32[]{:S(2)}) collective-permute-start(f32[128,128]{1,0:T(8,128)S(1)} %add.10.refs_0_), channel_id=1, source_target_pairs={{0,16},{4,20},{8,24},{12,28},{16,0},{20,4},{24,8},{28,12},{1,17},{... | collective-permute-start | bytes 196616 | tf_op jit(solution)/shard_map/all_gram/ppermute | solution.py:186
  14.9 0.0 collective-permute-done.5
  15.0 0.1 collective-permute-start.6
  15.0 1.6 %collective-permute-start.7 = (f32[25,8,128]{2,1,0:T(8,128)S(1)}, f32[25,8,128]{2,1,0:T(8,128)S(1)}, u32[]{:S(2)}, u32[]{:S(2)}) collective-permute-start(f32[25,8,128]{2,1,0:T(8,128)S(1)} %add.11.refs_5_), channel_id=1, source_target_pairs={{0,1},{1,0},{2,3},{3,2},{4,5},{5,4},{6,7},{7,6},{8,9},{9,8},{10,11... | collective-permute-start | bytes 307208 | tf_op jit(solution)/shard_map/other_half/ppermute | solution.py:182
  16.7 1.0 %collective-permute-done.3.refs_1_ = f32[128,128]{1,0:T(8,128)S(1)} collective-permute-done((f32[128,128]{1,0:T(8,128)S(1)}, f32[128,128]{1,0:T(8,128)S(1)}, u32[]{:S(2)}, u32[]{:S(2)}) %collective-permute-start.3) | collective-permute-done | bytes 65568 | tf_op jit(solution)/shard_map/all_gram/ppermute | solution.py:186
  17.7 0.0 collective-permute-done.4.refs_1_
  17.8 2.6 %collective-permute-done.7.refs_6_ = f32[25,8,128]{2,1,0:T(8,128)S(1)} collective-permute-done((f32[25,8,128]{2,1,0:T(8,128)S(1)}, f32[25,8,128]{2,1,0:T(8,128)S(1)}, u32[]{:S(2)}, u32[]{:S(2)}) %collective-permute-start.7) | collective-permute-done | bytes 102432 | tf_op jit(solution)/shard_map/other_half/ppermute | solution.py:182
  20.3 0.0 collective-permute-done.6.refs_3_
  20.4 2.9 %solve.1 = f32[24,128]{1,0:T(8,128)} custom-call(f32[512,128]{1,0:T(8,128)S(1)} %copy-done, f32[512,128]{1,0:T(8,128)S(1)} %collective-permute-done.4.refs_1_, f32[512,128]{1,0:T(8,128)S(1)} %collective-permute-done.second.refs_2_, f32[512,128]{1,0:T(8,128)S(1)} %collective-permute-done.6.refs_3_, bf16[128,256]{1,0:T(8,128)(2,1)S(1)} %base.1.refs_4_, ...), custom_call_target="tpu_custom_call" | custom-call | tf_op jit(solution)/shard_map/solve/pallas_call | solution.py:255
  (5 shorter events, 0.1 us)
Async XLA Ops:
  0.0 11.6 %copy-start = (f32[512,128]{1,0:T(8,128)S(1)}, f32[512,128]{1,0:T(8,128)}, u32[]{:S(2)}) copy-start(f32[512,128]{1,0:T(8,128)} %refs_0_.3) | copy-start | bytes 786436
  0.0 11.6 %collective-permute-start = (f32[512,128]{1,0:T(8,128)}, f32[512,128]{1,0:T(8,128)S(1)}, u32[]{:S(2)}, u32[]{:S(2)}) collective-permute-start(f32[512,128]{1,0:T(8,128)} %refs_0_.3), channel_id=1, source_target_pairs={{0,8},{4,12},{8,16},{12,20},{16,24},{20,28},{24,0},{28,4},{1,9},{5... | collective-permute-start | bytes 786440 | tf_op jit(solution)/shard_map/second_shard/ppermute | solution.py:186
  4.2 4.7 %collective-permute-start.1 = (f32[25,8,128]{2,1,0:T(8,128)S(1)}, f32[25,8,128]{2,1,0:T(8,128)S(1)}, u32[]{:S(2)}, u32[]{:S(2)}) collective-permute-start(f32[25,8,128]{2,1,0:T(8,128)S(1)} %get-tuple-element.13), channel_id=1, source_target_pairs={{0,1},{1,0},{2,3},{3,2},{4,5},{5,4},{6,7},{7,6},{8,9},{9,8},{10,11... | collective-permute-start | bytes 307208 | tf_op jit(solution)/shard_map/near_halves/ppermute | solution.py:182
  5.9 11.8 %collective-permute-start.4 = (f32[512,128]{1,0:T(8,128)}, f32[512,128]{1,0:T(8,128)S(1)}, u32[]{:S(2)}, u32[]{:S(2)}) collective-permute-start(f32[512,128]{1,0:T(8,128)} %refs_0_.3), channel_id=1, source_target_pairs={{0,4},{4,16},{8,12},{12,24},{16,20},{20,0},{24,28},{28,8},{1,5},{5... | collective-permute-start | bytes 786440 | tf_op jit(solution)/shard_map/first_shard/ppermute | solution.py:212
  9.0 6.0 %collective-permute-start.5 = (f32[25,8,128]{2,1,0:T(8,128)S(1)}, f32[25,8,128]{2,1,0:T(8,128)S(1)}, u32[]{:S(2)}, u32[]{:S(2)}) collective-permute-start(f32[25,8,128]{2,1,0:T(8,128)S(1)} %add.9), channel_id=1, source_target_pairs={{0,2},{1,3},{2,0},{3,1},{4,6},{5,7},{6,4},{7,5},{8,10},{9,11},{10,... | collective-permute-start | bytes 307208 | tf_op jit(solution)/shard_map/far_halves/ppermute | solution.py:186
  12.0 1.3 %collective-permute-start.2 = (f32[128,128]{1,0:T(8,128)S(1)}, f32[128,128]{1,0:T(8,128)S(1)}, u32[]{:S(2)}, u32[]{:S(2)}) collective-permute-start(f32[128,128]{1,0:T(8,128)S(1)} %gram.1), channel_id=1, source_target_pairs={{0,4},{4,0},{8,12},{12,8},{16,20},{20,16},{24,28},{28,24},{1,5},{5... | collective-permute-start | bytes 196616 | tf_op jit(solution)/shard_map/chip_gram/ppermute | solution.py:182
  13.4 4.3 %collective-permute-start.3 = (f32[128,128]{1,0:T(8,128)S(1)}, f32[128,128]{1,0:T(8,128)S(1)}, u32[]{:S(2)}, u32[]{:S(2)}) collective-permute-start(f32[128,128]{1,0:T(8,128)S(1)} %add.10.refs_0_), channel_id=1, source_target_pairs={{0,16},{4,20},{8,24},{12,28},{16,0},{20,4},{24,8},{28,12},{1,17},{... | collective-permute-start | bytes 196616 | tf_op jit(solution)/shard_map/all_gram/ppermute | solution.py:186
  15.0 5.4 %collective-permute-start.6 = (f32[512,128]{1,0:T(8,128)S(1)}, f32[512,128]{1,0:T(8,128)S(1)}, u32[]{:S(2)}, u32[]{:S(2)}) collective-permute-start(f32[512,128]{1,0:T(8,128)S(1)} %collective-permute-done.second.refs_2_), channel_id=1, source_target_pairs={{0,4},{4,0},{8,12},{12,8},{16,20},{20,16},{24,28},{28,24},{1,5},{5... | collective-permute-start | bytes 786440 | tf_op jit(solution)/shard_map/third_shard/ppermute | solution.py:182
  15.0 5.3 %collective-permute-start.7 = (f32[25,8,128]{2,1,0:T(8,128)S(1)}, f32[25,8,128]{2,1,0:T(8,128)S(1)}, u32[]{:S(2)}, u32[]{:S(2)}) collective-permute-start(f32[25,8,128]{2,1,0:T(8,128)S(1)} %add.11.refs_5_), channel_id=1, source_target_pairs={{0,1},{1,0},{2,3},{3,2},{4,5},{5,4},{6,7},{7,6},{8,9},{9,8},{10,11... | collective-permute-start | bytes 307208 | tf_op jit(solution)/shard_map/other_half/ppermute | solution.py:182

commit v6 on v5

--- a/solution.py
+++ b/solution.py
@@ -13,8 +13,8 @@
 RIDGE = 0.1
 VMEM_LIMIT = 16 * 2**20
 
-SUM_COST = 400_000_000
-BASE_COST = 1_800_000_000
+SUM_COST = 600000000
+BASE_COST = 1900000000
 
 SUB = 8
 LANES = 128
@@ -69,6 +69,12 @@
     refs[-1][...] = functools.reduce(jnp.add, [ref[...] for ref in refs[:-1]])
 
 
+def place_kernel(mine, other, low, high):
+    upper = lax.rem(lax.axis_index("split"), 2)
+    low[...] = jnp.where(upper == 1, other[...], mine[...])
+    high[...] = jnp.where(upper == 1, mine[...], other[...])
+
+
 def base_kernel(gram, out):
     rows = lax.broadcasted_iota(jnp.int32, gram.shape, 0)
     columns = lax.broadcasted_iota(jnp.int32, gram.shape, 1)
@@ -78,14 +84,13 @@
 
 def solve_kernel(item_blocks, half, *refs):
     shards = refs[:STEPS]
-    base_pair, keep, other, out, weights, wide, tall = refs[STEPS:]
+    base_pair, low, high, out, weights, wide, tall = refs[STEPS:]
     cells = STEPS * item_blocks
-    upper = lax.rem(lax.axis_index("split"), 2)
     users = USER_BLOCKS * SUB
     features = LANES
 
-    weights[pl.ds(upper * half, half)] = keep[...]
-    weights[pl.ds((1 - upper) * half, half)] = other[...]
+    weights[0:half] = low[...]
+    weights[half:] = high[...]
 
     for k in range(STEPS):
         high, low = split_parts(shards[k][...])
@@ -240,6 +245,18 @@
     with jax.named_scope("third_shard"):
         third = pair(ready, "item")
     gram, first = lax.optimization_barrier((gram, first))
+    with jax.named_scope("other_half"):
+        other = pair(total, "split")
+    other, gram = lax.optimization_barrier((other, gram))
+    low, high = pl.pallas_call(
+        place_kernel,
+        out_shape=[half_tiles] * 2,
+        in_specs=[vmem] * 2,
+        out_specs=[vmem] * 2,
+        compiler_params=params,
+        name="place",
+    )(total, other)
+
     base_pair = pl.pallas_call(
         base_kernel,
         out_shape=jax.ShapeDtypeStruct((features, 2 * features), jnp.bfloat16),
@@ -249,9 +266,6 @@
         cost_estimate=cost(BASE_COST),
         name="base",
     )(gram)
-    with jax.named_scope("other_half"):
-        other = pair(total, "split")
-
     return pl.pallas_call(
         functools.partial(solve_kernel, item_blocks, half),
         out_shape=jax.ShapeDtypeStruct((USER_BLOCKS * block_users, features), f32),
@@ -264,7 +278,7 @@
         ],
         compiler_params=params,
         name="solve",
-    )(item_emb, first, second, third, base_pair, total, other)
+    )(item_emb, first, second, third, base_pair, low, high)
 
 
 def solution(mesh):

time: 23.4 us -> 22.8 us (0.974)
  waiting for transfers between devices: 7.94 us -> 7.4 us
    ppermute x4, waiting for transfers between devices: 6.92 us -> 6.31 us  [pair(): lax.ppermute(value, axis, [(i, i ^ 1) for i in range(lax.axis_size(axis))])]
  transfers between devices with their start and end apart: 8 -> 8, of which waited for: 4 -> 4; matrix products, arithmetic and copies ran while one was open for 0% -> 0% of each run, Pallas kernels for 7% -> 8%
where the time goes in v6:
time: 22.8 us; the launch traced here: 22.7 us
  starting transfers between devices  10.5 us (46%)
  waiting for transfers between devices  7.4 us (32%)
  Pallas kernels  4.65 us (20%)
    ppermute x3, starting transfers between devices, shifted(): lax.ppermute(value, axis, [(i, (i + steps) % count) for i in range(count)])  7.17 us
    ppermute x4, waiting for transfers between devices, pair(): lax.ppermute(value, axis, [(i, i ^ 1) for i in range(lax.axis_size(axis))])  6.31 us
    ppermute x4, starting transfers between devices, pair(): lax.ppermute(value, axis, [(i, i ^ 1) for i in range(lax.axis_size(axis))])  3.35 us
    pallas_call x1, Pallas kernels, body(): pl.pallas_call(functools.partial(solve_kernel, item_blocks, half), out_sh...  2.92 us
    pallas_call x1, Pallas kernels, body(): pl.pallas_call(functools.partial(weights_kernel, item_blocks, half), out_...  1.29 us
    ppermute x3, waiting for transfers between devices, shifted(): lax.ppermute(value, axis, [(i, (i + steps) % count) for i in range(count)])  1.09 us
  transfers between devices with their start and end apart: 8, of which 4 were waited for; matrix products, arithmetic and copies ran while one was open for 0% of the time, Pallas kernels for 8%

profile of v6, /device:TPU:0, one launch (start us, length us, event | category | flops | bytes accessed | tf_op | source)
XLA Modules:
  0.0 22.7 jit_solution(14943268127271456214)
XLA Ops:
  0.0 0.0 copy-start
  0.0 2.9 %collective-permute-start = (f32[512,128]{1,0:T(8,128)}, f32[512,128]{1,0:T(8,128)S(1)}, u32[]{:S(2)}, u32[]{:S(2)}) collective-permute-start(f32[512,128]{1,0:T(8,128)} %refs_0_.3), channel_id=1, source_target_pairs={{0,8},{4,12},{8,16},{12,20},{16,24},{20,28},{24,0},{28,4},{1,9},{5... | collective-permute-start | bytes 786440 | tf_op jit(solution)/shard_map/second_shard/ppermute | solution.py:191
  2.9 1.3 %weights.1 = (f32[25,8,128]{2,1,0:T(8,128)S(1)}, f32[25,8,128]{2,1,0:T(8,128)S(1)}) custom-call(s32[1,1,4,16]{3,2,1,0:T(4,128)} %refs_0_.2, s32[1,1,4,16]{3,2,1,0:T(4,128)} %refs_1_.1, s32[1,1,4,16]{3,2,1,0:T(4,128)} %refs_2_.1, s32[1,1,4]{2,1,0:T(1,128)} %refs_3_.1, bf16[1,1,4,16,8,128]{5,4,3,2,1,0:T(8,128)(2,1)} %refs_4_.1), custom_call_target="tpu_custom_call" | custom-call | tf_op jit(solution)/shard_map/weights/pallas_call | solution.py:197
  4.2 1.6 %collective-permute-start.1 = (f32[25,8,128]{2,1,0:T(8,128)S(1)}, f32[25,8,128]{2,1,0:T(8,128)S(1)}, u32[]{:S(2)}, u32[]{:S(2)}) collective-permute-start(f32[25,8,128]{2,1,0:T(8,128)S(1)} %get-tuple-element.17), channel_id=1, source_target_pairs={{0,1},{1,0},{2,3},{3,2},{4,5},{5,4},{6,7},{7,6},{8,9},{9,8},{10,11... | collective-permute-start | bytes 307208 | tf_op jit(solution)/shard_map/near_halves/ppermute | solution.py:187
  5.9 0.0 collective-permute-start.4
  5.9 3.1 %collective-permute-done.1 = f32[25,8,128]{2,1,0:T(8,128)S(1)} collective-permute-done((f32[25,8,128]{2,1,0:T(8,128)S(1)}, f32[25,8,128]{2,1,0:T(8,128)S(1)}, u32[]{:S(2)}, u32[]{:S(2)}) %collective-permute-start.1) | collective-permute-done | bytes 102432 | tf_op jit(solution)/shard_map/near_halves/ppermute | solution.py:187
  9.0 2.6 %collective-permute-start.5 = (f32[25,8,128]{2,1,0:T(8,128)S(1)}, f32[25,8,128]{2,1,0:T(8,128)S(1)}, u32[]{:S(2)}, u32[]{:S(2)}) collective-permute-start(f32[25,8,128]{2,1,0:T(8,128)S(1)} %add.9), channel_id=1, source_target_pairs={{0,2},{1,3},{2,0},{3,1},{4,6},{5,7},{6,4},{7,5},{8,10},{9,11},{10,... | collective-permute-start | bytes 307208 | tf_op jit(solution)/shard_map/far_halves/ppermute | solution.py:191
  11.6 0.0 collective-permute-done.second.refs_2_
  11.6 0.0 copy-done
  11.6 0.4 %gram.1 = f32[128,128]{1,0:T(8,128)S(1)} custom-call(f32[512,128]{1,0:T(8,128)S(1)} %copy-done, f32[512,128]{1,0:T(8,128)S(1)} %collective-permute-done.second.refs_2_), custom_call_target="tpu_custom_call" | custom-call | tf_op jit(solution)/shard_map/gram/pallas_call | solution.py:223
  12.0 0.1 collective-permute-start.2
  12.1 1.2 %collective-permute-done.2 = f32[128,128]{1,0:T(8,128)S(1)} collective-permute-done((f32[128,128]{1,0:T(8,128)S(1)}, f32[128,128]{1,0:T(8,128)S(1)}, u32[]{:S(2)}, u32[]{:S(2)}) %collective-permute-start.2) | collective-permute-done | bytes 65568 | tf_op jit(solution)/shard_map/chip_gram/ppermute | solution.py:187
  13.4 1.6 %collective-permute-start.3 = (f32[128,128]{1,0:T(8,128)S(1)}, f32[128,128]{1,0:T(8,128)S(1)}, u32[]{:S(2)}, u32[]{:S(2)}) collective-permute-start(f32[128,128]{1,0:T(8,128)S(1)} %add.10.refs_0_), channel_id=1, source_target_pairs={{0,16},{4,20},{8,24},{12,28},{16,0},{20,4},{24,8},{28,12},{1,17},{... | collective-permute-start | bytes 196616 | tf_op jit(solution)/shard_map/all_gram/ppermute | solution.py:191
  14.9 0.0 collective-permute-done.5
  15.0 1.6 %collective-permute-start.7 = (f32[25,8,128]{2,1,0:T(8,128)S(1)}, f32[25,8,128]{2,1,0:T(8,128)S(1)}, u32[]{:S(2)}, u32[]{:S(2)}) collective-permute-start(f32[25,8,128]{2,1,0:T(8,128)S(1)} %add.11.mine), channel_id=1, source_target_pairs={{0,1},{1,0},{2,3},{3,2},{4,5},{5,4},{6,7},{7,6},{8,9},{9,8},{10,11... | collective-permute-start | bytes 307208 | tf_op jit(solution)/shard_map/other_half/ppermute | solution.py:187
  16.6 0.0 collective-permute-start.6
  16.6 1.1 %collective-permute-done.3.refs_1_ = f32[128,128]{1,0:T(8,128)S(1)} collective-permute-done((f32[128,128]{1,0:T(8,128)S(1)}, f32[128,128]{1,0:T(8,128)S(1)}, u32[]{:S(2)}, u32[]{:S(2)}) %collective-permute-start.3) | collective-permute-done | bytes 65568 | tf_op jit(solution)/shard_map/all_gram/ppermute | solution.py:191
  17.7 0.0 collective-permute-done.4.refs_1_
  17.7 2.0 %collective-permute-done.7.other = f32[25,8,128]{2,1,0:T(8,128)S(1)} collective-permute-done((f32[25,8,128]{2,1,0:T(8,128)S(1)}, f32[25,8,128]{2,1,0:T(8,128)S(1)}, u32[]{:S(2)}, u32[]{:S(2)}) %collective-permute-start.7) | collective-permute-done | bytes 102432 | tf_op jit(solution)/shard_map/other_half/ppermute | solution.py:187
  19.8 0.0 collective-permute-done.6.refs_3_
  19.8 2.9 %solve.1 = f32[24,128]{1,0:T(8,128)} custom-call(f32[512,128]{1,0:T(8,128)S(1)} %copy-done, f32[512,128]{1,0:T(8,128)S(1)} %collective-permute-done.4.refs_1_, f32[512,128]{1,0:T(8,128)S(1)} %collective-permute-done.second.refs_2_, f32[512,128]{1,0:T(8,128)S(1)} %collective-permute-done.6.refs_3_, bf16[128,256]{1,0:T(8,128)(2,1)S(1)} %base.1.refs_4_, ...), custom_call_target="tpu_custom_call" | custom-call | tf_op jit(solution)/shard_map/solve/pallas_call | solution.py:269
  (6 shorter events, 0.1 us)
Async XLA Ops:
  0.0 11.6 %copy-start = (f32[512,128]{1,0:T(8,128)S(1)}, f32[512,128]{1,0:T(8,128)}, u32[]{:S(2)}) copy-start(f32[512,128]{1,0:T(8,128)} %refs_0_.3) | copy-start | bytes 786436
  0.0 11.6 %collective-permute-start = (f32[512,128]{1,0:T(8,128)}, f32[512,128]{1,0:T(8,128)S(1)}, u32[]{:S(2)}, u32[]{:S(2)}) collective-permute-start(f32[512,128]{1,0:T(8,128)} %refs_0_.3), channel_id=1, source_target_pairs={{0,8},{4,12},{8,16},{12,20},{16,24},{20,28},{24,0},{28,4},{1,9},{5... | collective-permute-start | bytes 786440 | tf_op jit(solution)/shard_map/second_shard/ppermute | solution.py:191
  4.2 4.7 %collective-permute-start.1 = (f32[25,8,128]{2,1,0:T(8,128)S(1)}, f32[25,8,128]{2,1,0:T(8,128)S(1)}, u32[]{:S(2)}, u32[]{:S(2)}) collective-permute-start(f32[25,8,128]{2,1,0:T(8,128)S(1)} %get-tuple-element.17), channel_id=1, source_target_pairs={{0,1},{1,0},{2,3},{3,2},{4,5},{5,4},{6,7},{7,6},{8,9},{9,8},{10,11... | collective-permute-start | bytes 307208 | tf_op jit(solution)/shard_map/near_halves/ppermute | solution.py:187
  5.9 11.8 %collective-permute-start.4 = (f32[512,128]{1,0:T(8,128)}, f32[512,128]{1,0:T(8,128)S(1)}, u32[]{:S(2)}, u32[]{:S(2)}) collective-permute-start(f32[512,128]{1,0:T(8,128)} %refs_0_.3), channel_id=1, source_target_pairs={{0,4},{4,16},{8,12},{12,24},{16,20},{20,0},{24,28},{28,8},{1,5},{5... | collective-permute-start | bytes 786440 | tf_op jit(solution)/shard_map/first_shard/ppermute | solution.py:217
  9.0 6.0 %collective-permute-start.5 = (f32[25,8,128]{2,1,0:T(8,128)S(1)}, f32[25,8,128]{2,1,0:T(8,128)S(1)}, u32[]{:S(2)}, u32[]{:S(2)}) collective-permute-start(f32[25,8,128]{2,1,0:T(8,128)S(1)} %add.9), channel_id=1, source_target_pairs={{0,2},{1,3},{2,0},{3,1},{4,6},{5,7},{6,4},{7,5},{8,10},{9,11},{10,... | collective-permute-start | bytes 307208 | tf_op jit(solution)/shard_map/far_halves/ppermute | solution.py:191
  12.0 1.3 %collective-permute-start.2 = (f32[128,128]{1,0:T(8,128)S(1)}, f32[128,128]{1,0:T(8,128)S(1)}, u32[]{:S(2)}, u32[]{:S(2)}) collective-permute-start(f32[128,128]{1,0:T(8,128)S(1)} %gram.1), channel_id=1, source_target_pairs={{0,4},{4,0},{8,12},{12,8},{16,20},{20,16},{24,28},{28,24},{1,5},{5... | collective-permute-start | bytes 196616 | tf_op jit(solution)/shard_map/chip_gram/ppermute | solution.py:187
  13.4 4.3 %collective-permute-start.3 = (f32[128,128]{1,0:T(8,128)S(1)}, f32[128,128]{1,0:T(8,128)S(1)}, u32[]{:S(2)}, u32[]{:S(2)}) collective-permute-start(f32[128,128]{1,0:T(8,128)S(1)} %add.10.refs_0_), channel_id=1, source_target_pairs={{0,16},{4,20},{8,24},{12,28},{16,0},{20,4},{24,8},{28,12},{1,17},{... | collective-permute-start | bytes 196616 | tf_op jit(solution)/shard_map/all_gram/ppermute | solution.py:191
  15.0 4.7 %collective-permute-start.7 = (f32[25,8,128]{2,1,0:T(8,128)S(1)}, f32[25,8,128]{2,1,0:T(8,128)S(1)}, u32[]{:S(2)}, u32[]{:S(2)}) collective-permute-start(f32[25,8,128]{2,1,0:T(8,128)S(1)} %add.11.mine), channel_id=1, source_target_pairs={{0,1},{1,0},{2,3},{3,2},{4,5},{5,4},{6,7},{7,6},{8,9},{9,8},{10,11... | collective-permute-start | bytes 307208 | tf_op jit(solution)/shard_map/other_half/ppermute | solution.py:187
  16.6 3.1 %collective-permute-start.6 = (f32[512,128]{1,0:T(8,128)S(1)}, f32[512,128]{1,0:T(8,128)S(1)}, u32[]{:S(2)}, u32[]{:S(2)}) collective-permute-start(f32[512,128]{1,0:T(8,128)S(1)} %collective-permute-done.second.refs_2_), channel_id=1, source_target_pairs={{0,4},{4,0},{8,12},{12,8},{16,20},{20,16},{24,28},{28,24},{1,5},{5... | collective-permute-start | bytes 786440 | tf_op jit(solution)/shard_map/third_shard/ppermute | solution.py:187

commit v7 on v6

--- a/solution.py
+++ b/solution.py
@@ -84,13 +84,13 @@
 
 def solve_kernel(item_blocks, half, *refs):
     shards = refs[:STEPS]
-    base_pair, low, high, out, weights, wide, tall = refs[STEPS:]
+    base_pair, lower, upper, out, wide, tall = refs[STEPS:]
     cells = STEPS * item_blocks
     users = USER_BLOCKS * SUB
     features = LANES
 
-    weights[0:half] = low[...]
-    weights[half:] = high[...]
+    def tile(index):
+        return lower[index] if index < half else upper[index - half]
 
     for k in range(STEPS):
         high, low = split_parts(shards[k][...])
@@ -100,13 +100,13 @@
     def conf_of(k):
         return jnp.concatenate(
             [
-                jnp.concatenate([weights[ub * cells + k * item_blocks + i] for i in range(item_blocks)], axis=1)
+                jnp.concatenate([tile(ub * cells + k * item_blocks + i) for i in range(item_blocks)], axis=1)
                 for ub in range(USER_BLOCKS)
             ],
             axis=0,
         )
 
-    recency_sums = weights[USER_BLOCKS * cells]
+    recency_sums = tile(USER_BLOCKS * cells)
 
     def count_of(k):
         return jnp.concatenate(
@@ -135,8 +135,8 @@
 
     right = folded(sum(back(conf_of(k) + count_of(k), k) for k in range(STEPS)))
 
-    def scores_of(direction):
-        high, low = split_parts(direction)
+    def scores_of(value):
+        high, low = split_parts(value)
         left = jnp.concatenate(
             [jnp.concatenate([high, high], axis=1), jnp.concatenate([low, low], axis=1)], axis=0
         ).astype(jnp.bfloat16)
@@ -152,8 +152,8 @@
     residual = right
     direction = right
     norm_now = jnp.sum(residual * residual, axis=1, keepdims=True)
+    through, scores = scores_of(right)
     for iteration in range(CG_ITERS):
-        through, scores = scores_of(direction)
         weighted = [scores[k] * confs[k] for k in range(STEPS)]
         curve = direction * through
         for k in range(STEPS):
@@ -166,7 +166,11 @@
             image = through + folded(sum(back(weighted[k], k) for k in range(STEPS)))
             residual = residual - step * image
             norm_next = jnp.sum(residual * residual, axis=1, keepdims=True)
-            direction = residual + (norm_next / norm_now) * direction
+            through_next, scores_next = scores_of(residual)
+            ratio = norm_next / norm_now
+            direction = residual + ratio * direction
+            through = through_next + ratio * through
+            scores = [n + ratio * s for n, s in zip(scores_next, scores)]
             norm_now = norm_next
     out[...] = answer
 
@@ -272,7 +276,6 @@
         in_specs=[vmem] * (STEPS + 3),
         out_specs=vmem,
         scratch_shapes=[
-            pltpu.VMEM((2 * half, SUB, LANES), f32),
             pltpu.VMEM((STEPS, 2 * features, rows), jnp.bfloat16),
             pltpu.VMEM((STEPS, rows, 2 * features), jnp.bfloat16),
         ],

time: 22.8 us -> 22.7 us (level)
  no operation moved by 1% of the time
where the time goes in v7:
time: 22.7 us; the launch traced here: 22.5 us
  starting transfers between devices  10.5 us (46%)
  waiting for transfers between devices  7.39 us (33%)
  Pallas kernels  4.49 us (20%)
    ppermute x3, starting transfers between devices, shifted(): lax.ppermute(value, axis, [(i, (i + steps) % count) for i in range(count)])  7.18 us
    ppermute x4, waiting for transfers between devices, pair(): lax.ppermute(value, axis, [(i, i ^ 1) for i in range(lax.axis_size(axis))])  6.31 us
    ppermute x4, starting transfers between devices, pair(): lax.ppermute(value, axis, [(i, i ^ 1) for i in range(lax.axis_size(axis))])  3.36 us
    pallas_call x1, Pallas kernels, body(): pl.pallas_call(functools.partial(solve_kernel, item_blocks, half), out_sh...  2.76 us
    pallas_call x1, Pallas kernels, body(): pl.pallas_call(functools.partial(weights_kernel, item_blocks, half), out_...  1.28 us
    ppermute x3, waiting for transfers between devices, shifted(): lax.ppermute(value, axis, [(i, (i + steps) % count) for i in range(count)])  1.09 us
  transfers between devices with their start and end apart: 8, of which 4 were waited for; matrix products, arithmetic and copies ran while one was open for 0% of the time, Pallas kernels for 8%

profile of v7, /device:TPU:0, one launch (start us, length us, event | category | flops | bytes accessed | tf_op | source)
XLA Modules:
  0.0 22.5 jit_solution(8188402594743248038)
XLA Ops:
  0.0 0.0 copy-start
  0.0 2.9 %collective-permute-start = (f32[512,128]{1,0:T(8,128)}, f32[512,128]{1,0:T(8,128)S(1)}, u32[]{:S(2)}, u32[]{:S(2)}) collective-permute-start(f32[512,128]{1,0:T(8,128)} %refs_0_.3), channel_id=1, source_target_pairs={{0,8},{4,12},{8,16},{12,20},{16,24},{20,28},{24,0},{28,4},{1,9},{5... | collective-permute-start | bytes 786440 | tf_op jit(solution)/shard_map/second_shard/ppermute | solution.py:195
  2.9 1.3 %weights.1 = (f32[25,8,128]{2,1,0:T(8,128)S(1)}, f32[25,8,128]{2,1,0:T(8,128)S(1)}) custom-call(s32[1,1,4,16]{3,2,1,0:T(4,128)} %refs_0_.2, s32[1,1,4,16]{3,2,1,0:T(4,128)} %refs_1_.1, s32[1,1,4,16]{3,2,1,0:T(4,128)} %refs_2_.1, s32[1,1,4]{2,1,0:T(1,128)} %refs_3_.1, bf16[1,1,4,16,8,128]{5,4,3,2,1,0:T(8,128)(2,1)} %refs_4_.1), custom_call_target="tpu_custom_call" | custom-call | tf_op jit(solution)/shard_map/weights/pallas_call | solution.py:201
  4.2 1.6 %collective-permute-start.1 = (f32[25,8,128]{2,1,0:T(8,128)S(1)}, f32[25,8,128]{2,1,0:T(8,128)S(1)}, u32[]{:S(2)}, u32[]{:S(2)}) collective-permute-start(f32[25,8,128]{2,1,0:T(8,128)S(1)} %get-tuple-element.17), channel_id=1, source_target_pairs={{0,1},{1,0},{2,3},{3,2},{4,5},{5,4},{6,7},{7,6},{8,9},{9,8},{10,11... | collective-permute-start | bytes 307208 | tf_op jit(solution)/shard_map/near_halves/ppermute | solution.py:191
  5.9 0.0 collective-permute-start.4
  5.9 3.1 %collective-permute-done.1 = f32[25,8,128]{2,1,0:T(8,128)S(1)} collective-permute-done((f32[25,8,128]{2,1,0:T(8,128)S(1)}, f32[25,8,128]{2,1,0:T(8,128)S(1)}, u32[]{:S(2)}, u32[]{:S(2)}) %collective-permute-start.1) | collective-permute-done | bytes 102432 | tf_op jit(solution)/shard_map/near_halves/ppermute | solution.py:191
  9.0 2.7 %collective-permute-start.5 = (f32[25,8,128]{2,1,0:T(8,128)S(1)}, f32[25,8,128]{2,1,0:T(8,128)S(1)}, u32[]{:S(2)}, u32[]{:S(2)}) collective-permute-start(f32[25,8,128]{2,1,0:T(8,128)S(1)} %add.9), channel_id=1, source_target_pairs={{0,2},{1,3},{2,0},{3,1},{4,6},{5,7},{6,4},{7,5},{8,10},{9,11},{10,... | collective-permute-start | bytes 307208 | tf_op jit(solution)/shard_map/far_halves/ppermute | solution.py:195
  11.6 0.0 collective-permute-done.second.refs_2_
  11.6 0.0 copy-done
  11.6 0.4 %gram.1 = f32[128,128]{1,0:T(8,128)S(1)} custom-call(f32[512,128]{1,0:T(8,128)S(1)} %copy-done, f32[512,128]{1,0:T(8,128)S(1)} %collective-permute-done.second.refs_2_), custom_call_target="tpu_custom_call" | custom-call | tf_op jit(solution)/shard_map/gram/pallas_call | solution.py:227
  12.0 0.1 collective-permute-start.2
  12.1 1.2 %collective-permute-done.2 = f32[128,128]{1,0:T(8,128)S(1)} collective-permute-done((f32[128,128]{1,0:T(8,128)S(1)}, f32[128,128]{1,0:T(8,128)S(1)}, u32[]{:S(2)}, u32[]{:S(2)}) %collective-permute-start.2) | collective-permute-done | bytes 65568 | tf_op jit(solution)/shard_map/chip_gram/ppermute | solution.py:191
  13.4 1.6 %collective-permute-start.3 = (f32[128,128]{1,0:T(8,128)S(1)}, f32[128,128]{1,0:T(8,128)S(1)}, u32[]{:S(2)}, u32[]{:S(2)}) collective-permute-start(f32[128,128]{1,0:T(8,128)S(1)} %add.10.refs_0_), channel_id=1, source_target_pairs={{0,16},{4,20},{8,24},{12,28},{16,0},{20,4},{24,8},{28,12},{1,17},{... | collective-permute-start | bytes 196616 | tf_op jit(solution)/shard_map/all_gram/ppermute | solution.py:195
  14.9 0.0 collective-permute-done.5
  15.0 1.6 %collective-permute-start.7 = (f32[25,8,128]{2,1,0:T(8,128)S(1)}, f32[25,8,128]{2,1,0:T(8,128)S(1)}, u32[]{:S(2)}, u32[]{:S(2)}) collective-permute-start(f32[25,8,128]{2,1,0:T(8,128)S(1)} %add.11.mine), channel_id=1, source_target_pairs={{0,1},{1,0},{2,3},{3,2},{4,5},{5,4},{6,7},{7,6},{8,9},{9,8},{10,11... | collective-permute-start | bytes 307208 | tf_op jit(solution)/shard_map/other_half/ppermute | solution.py:191
  16.6 0.0 collective-permute-start.6
  16.6 1.1 %collective-permute-done.3.refs_1_ = f32[128,128]{1,0:T(8,128)S(1)} collective-permute-done((f32[128,128]{1,0:T(8,128)S(1)}, f32[128,128]{1,0:T(8,128)S(1)}, u32[]{:S(2)}, u32[]{:S(2)}) %collective-permute-start.3) | collective-permute-done | bytes 65568 | tf_op jit(solution)/shard_map/all_gram/ppermute | solution.py:195
  17.7 0.0 collective-permute-done.4.refs_1_
  17.7 2.0 %collective-permute-done.7.other = f32[25,8,128]{2,1,0:T(8,128)S(1)} collective-permute-done((f32[25,8,128]{2,1,0:T(8,128)S(1)}, f32[25,8,128]{2,1,0:T(8,128)S(1)}, u32[]{:S(2)}, u32[]{:S(2)}) %collective-permute-start.7) | collective-permute-done | bytes 102432 | tf_op jit(solution)/shard_map/other_half/ppermute | solution.py:191
  19.8 0.0 collective-permute-done.6.refs_3_
  19.8 2.8 %solve.1 = f32[24,128]{1,0:T(8,128)} custom-call(f32[512,128]{1,0:T(8,128)S(1)} %copy-done, f32[512,128]{1,0:T(8,128)S(1)} %collective-permute-done.4.refs_1_, f32[512,128]{1,0:T(8,128)S(1)} %collective-permute-done.second.refs_2_, f32[512,128]{1,0:T(8,128)S(1)} %collective-permute-done.6.refs_3_, bf16[128,256]{1,0:T(8,128)(2,1)S(1)} %base.1.refs_4_, ...), custom_call_target="tpu_custom_call" | custom-call | tf_op jit(solution)/shard_map/solve/pallas_call | solution.py:273
  (6 shorter events, 0.1 us)
Async XLA Ops:
  0.0 11.6 %copy-start = (f32[512,128]{1,0:T(8,128)S(1)}, f32[512,128]{1,0:T(8,128)}, u32[]{:S(2)}) copy-start(f32[512,128]{1,0:T(8,128)} %refs_0_.3) | copy-start | bytes 786436
  0.0 11.6 %collective-permute-start = (f32[512,128]{1,0:T(8,128)}, f32[512,128]{1,0:T(8,128)S(1)}, u32[]{:S(2)}, u32[]{:S(2)}) collective-permute-start(f32[512,128]{1,0:T(8,128)} %refs_0_.3), channel_id=1, source_target_pairs={{0,8},{4,12},{8,16},{12,20},{16,24},{20,28},{24,0},{28,4},{1,9},{5... | collective-permute-start | bytes 786440 | tf_op jit(solution)/shard_map/second_shard/ppermute | solution.py:195
  4.2 4.7 %collective-permute-start.1 = (f32[25,8,128]{2,1,0:T(8,128)S(1)}, f32[25,8,128]{2,1,0:T(8,128)S(1)}, u32[]{:S(2)}, u32[]{:S(2)}) collective-permute-start(f32[25,8,128]{2,1,0:T(8,128)S(1)} %get-tuple-element.17), channel_id=1, source_target_pairs={{0,1},{1,0},{2,3},{3,2},{4,5},{5,4},{6,7},{7,6},{8,9},{9,8},{10,11... | collective-permute-start | bytes 307208 | tf_op jit(solution)/shard_map/near_halves/ppermute | solution.py:191
  5.9 11.8 %collective-permute-start.4 = (f32[512,128]{1,0:T(8,128)}, f32[512,128]{1,0:T(8,128)S(1)}, u32[]{:S(2)}, u32[]{:S(2)}) collective-permute-start(f32[512,128]{1,0:T(8,128)} %refs_0_.3), channel_id=1, source_target_pairs={{0,4},{4,16},{8,12},{12,24},{16,20},{20,0},{24,28},{28,8},{1,5},{5... | collective-permute-start | bytes 786440 | tf_op jit(solution)/shard_map/first_shard/ppermute | solution.py:221
  9.0 6.0 %collective-permute-start.5 = (f32[25,8,128]{2,1,0:T(8,128)S(1)}, f32[25,8,128]{2,1,0:T(8,128)S(1)}, u32[]{:S(2)}, u32[]{:S(2)}) collective-permute-start(f32[25,8,128]{2,1,0:T(8,128)S(1)} %add.9), channel_id=1, source_target_pairs={{0,2},{1,3},{2,0},{3,1},{4,6},{5,7},{6,4},{7,5},{8,10},{9,11},{10,... | collective-permute-start | bytes 307208 | tf_op jit(solution)/shard_map/far_halves/ppermute | solution.py:195
  12.0 1.3 %collective-permute-start.2 = (f32[128,128]{1,0:T(8,128)S(1)}, f32[128,128]{1,0:T(8,128)S(1)}, u32[]{:S(2)}, u32[]{:S(2)}) collective-permute-start(f32[128,128]{1,0:T(8,128)S(1)} %gram.1), channel_id=1, source_target_pairs={{0,4},{4,0},{8,12},{12,8},{16,20},{20,16},{24,28},{28,24},{1,5},{5... | collective-permute-start | bytes 196616 | tf_op jit(solution)/shard_map/chip_gram/ppermute | solution.py:191
  13.4 4.3 %collective-permute-start.3 = (f32[128,128]{1,0:T(8,128)S(1)}, f32[128,128]{1,0:T(8,128)S(1)}, u32[]{:S(2)}, u32[]{:S(2)}) collective-permute-start(f32[128,128]{1,0:T(8,128)S(1)} %add.10.refs_0_), channel_id=1, source_target_pairs={{0,16},{4,20},{8,24},{12,28},{16,0},{20,4},{24,8},{28,12},{1,17},{... | collective-permute-start | bytes 196616 | tf_op jit(solution)/shard_map/all_gram/ppermute | solution.py:195
  15.0 4.7 %collective-permute-start.7 = (f32[25,8,128]{2,1,0:T(8,128)S(1)}, f32[25,8,128]{2,1,0:T(8,128)S(1)}, u32[]{:S(2)}, u32[]{:S(2)}) collective-permute-start(f32[25,8,128]{2,1,0:T(8,128)S(1)} %add.11.mine), channel_id=1, source_target_pairs={{0,1},{1,0},{2,3},{3,2},{4,5},{5,4},{6,7},{7,6},{8,9},{9,8},{10,11... | collective-permute-start | bytes 307208 | tf_op jit(solution)/shard_map/other_half/ppermute | solution.py:191
  16.6 3.2 %collective-permute-start.6 = (f32[512,128]{1,0:T(8,128)S(1)}, f32[512,128]{1,0:T(8,128)S(1)}, u32[]{:S(2)}, u32[]{:S(2)}) collective-permute-start(f32[512,128]{1,0:T(8,128)S(1)} %collective-permute-done.second.refs_2_), channel_id=1, source_target_pairs={{0,4},{4,0},{8,12},{12,8},{16,20},{20,16},{24,28},{28,24},{1,5},{5... | collective-permute-start | bytes 786440 | tf_op jit(solution)/shard_map/third_shard/ppermute | solution.py:191

commit v8 on v7

--- a/solution.py
+++ b/solution.py
@@ -88,13 +88,14 @@
     cells = STEPS * item_blocks
     users = USER_BLOCKS * SUB
     features = LANES
+    rows = shards[0].shape[0]
 
     def tile(index):
         return lower[index] if index < half else upper[index - half]
 
     for k in range(STEPS):
         high, low = split_parts(shards[k][...])
-        tall[k] = jnp.concatenate([high, low], axis=1).astype(jnp.bfloat16)
+        tall[k * rows : (k + 1) * rows] = jnp.concatenate([high, low], axis=1).astype(jnp.bfloat16)
         wide[k] = jnp.concatenate([high.T, low.T], axis=0).astype(jnp.bfloat16)
 
     def conf_of(k):
@@ -130,10 +131,11 @@
     def folded(pair):
         return (pair[:users, :features] + pair[:users, features:]) + (pair[users:, :features] + pair[users:, features:])
 
-    def back(value, k):
-        return jnp.dot(stacked(value), tall[k], preferred_element_type=jnp.float32)
-
-    right = folded(sum(back(conf_of(k) + count_of(k), k) for k in range(STEPS)))
+    def back(values):
+        left = jnp.concatenate([stacked(value) for value in values], axis=1)
+        return folded(jnp.dot(left, tall[...], preferred_element_type=jnp.float32))
+
+    right = back([conf_of(k) + count_of(k) for k in range(STEPS)])
 
     def scores_of(value):
         high, low = split_parts(value)
@@ -163,7 +165,7 @@
         step = norm_now / jnp.sum(curve, axis=1, keepdims=True)
         answer = answer + step * direction
         if iteration + 1 < CG_ITERS:
-            image = through + folded(sum(back(weighted[k], k) for k in range(STEPS)))
+            image = through + back(weighted)
             residual = residual - step * image
             norm_next = jnp.sum(residual * residual, axis=1, keepdims=True)
             through_next, scores_next = scores_of(residual)
@@ -277,7 +279,7 @@
         out_specs=vmem,
         scratch_shapes=[
             pltpu.VMEM((STEPS, 2 * features, rows), jnp.bfloat16),
-            pltpu.VMEM((STEPS, rows, 2 * features), jnp.bfloat16),
+            pltpu.VMEM((STEPS * rows, 2 * features), jnp.bfloat16),
         ],
         compiler_params=params,
         name="solve",

time: 22.7 us -> 22.6 us (level)
  no operation moved by 1% of the time
where the time goes in v8:
time: 22.6 us; the launch traced here: 22.5 us
  starting transfers between devices  10.6 us (47%)
  waiting for transfers between devices  7.38 us (33%)
  Pallas kernels  4.42 us (20%)
    ppermute x3, starting transfers between devices, shifted(): lax.ppermute(value, axis, [(i, (i + steps) % count) for i in range(count)])  7.18 us
    ppermute x4, waiting for transfers between devices, pair(): lax.ppermute(value, axis, [(i, i ^ 1) for i in range(lax.axis_size(axis))])  6.29 us
    ppermute x4, starting transfers between devices, pair(): lax.ppermute(value, axis, [(i, i ^ 1) for i in range(lax.axis_size(axis))])  3.37 us
    pallas_call x1, Pallas kernels, body(): pl.pallas_call(functools.partial(solve_kernel, item_blocks, half), out_sh...  2.7 us
    pallas_call x1, Pallas kernels, body(): pl.pallas_call(functools.partial(weights_kernel, item_blocks, half), out_...  1.28 us
    ppermute x3, waiting for transfers between devices, shifted(): lax.ppermute(value, axis, [(i, (i + steps) % count) for i in range(count)])  1.09 us
  transfers between devices with their start and end apart: 8, of which 4 were waited for; matrix products, arithmetic and copies ran while one was open for 0% of the time, Pallas kernels for 8%

profile of v8, /device:TPU:0, one launch (start us, length us, event | category | flops | bytes accessed | tf_op | source)
XLA Modules:
  0.0 22.5 jit_solution(17566970476468892703)
XLA Ops:
  0.0 0.0 copy-start
  0.0 2.9 %collective-permute-start = (f32[512,128]{1,0:T(8,128)}, f32[512,128]{1,0:T(8,128)S(1)}, u32[]{:S(2)}, u32[]{:S(2)}) collective-permute-start(f32[512,128]{1,0:T(8,128)} %refs_0_.3), channel_id=1, source_target_pairs={{0,8},{4,12},{8,16},{12,20},{16,24},{20,28},{24,0},{28,4},{1,9},{5... | collective-permute-start | bytes 786440 | tf_op jit(solution)/shard_map/second_shard/ppermute | solution.py:197
  2.9 1.3 %weights.1 = (f32[25,8,128]{2,1,0:T(8,128)S(1)}, f32[25,8,128]{2,1,0:T(8,128)S(1)}) custom-call(s32[1,1,4,16]{3,2,1,0:T(4,128)} %refs_0_.2, s32[1,1,4,16]{3,2,1,0:T(4,128)} %refs_1_.1, s32[1,1,4,16]{3,2,1,0:T(4,128)} %refs_2_.1, s32[1,1,4]{2,1,0:T(1,128)} %refs_3_.1, bf16[1,1,4,16,8,128]{5,4,3,2,1,0:T(8,128)(2,1)} %refs_4_.1), custom_call_target="tpu_custom_call" | custom-call | tf_op jit(solution)/shard_map/weights/pallas_call | solution.py:203
  4.2 1.7 %collective-permute-start.1 = (f32[25,8,128]{2,1,0:T(8,128)S(1)}, f32[25,8,128]{2,1,0:T(8,128)S(1)}, u32[]{:S(2)}, u32[]{:S(2)}) collective-permute-start(f32[25,8,128]{2,1,0:T(8,128)S(1)} %get-tuple-element.17), channel_id=1, source_target_pairs={{0,1},{1,0},{2,3},{3,2},{4,5},{5,4},{6,7},{7,6},{8,9},{9,8},{10,11... | collective-permute-start | bytes 307208 | tf_op jit(solution)/shard_map/near_halves/ppermute | solution.py:193
  5.9 0.0 collective-permute-start.4
  5.9 3.1 %collective-permute-done.1 = f32[25,8,128]{2,1,0:T(8,128)S(1)} collective-permute-done((f32[25,8,128]{2,1,0:T(8,128)S(1)}, f32[25,8,128]{2,1,0:T(8,128)S(1)}, u32[]{:S(2)}, u32[]{:S(2)}) %collective-permute-start.1) | collective-permute-done | bytes 102432 | tf_op jit(solution)/shard_map/near_halves/ppermute | solution.py:193
  9.0 2.7 %collective-permute-start.5 = (f32[25,8,128]{2,1,0:T(8,128)S(1)}, f32[25,8,128]{2,1,0:T(8,128)S(1)}, u32[]{:S(2)}, u32[]{:S(2)}) collective-permute-start(f32[25,8,128]{2,1,0:T(8,128)S(1)} %add.9), channel_id=1, source_target_pairs={{0,2},{1,3},{2,0},{3,1},{4,6},{5,7},{6,4},{7,5},{8,10},{9,11},{10,... | collective-permute-start | bytes 307208 | tf_op jit(solution)/shard_map/far_halves/ppermute | solution.py:197
  11.6 0.0 collective-permute-done.second.refs_2_
  11.6 0.0 copy-done
  11.6 0.4 %gram.1 = f32[128,128]{1,0:T(8,128)S(1)} custom-call(f32[512,128]{1,0:T(8,128)S(1)} %copy-done, f32[512,128]{1,0:T(8,128)S(1)} %collective-permute-done.second.refs_2_), custom_call_target="tpu_custom_call" | custom-call | tf_op jit(solution)/shard_map/gram/pallas_call | solution.py:229
  12.0 0.1 collective-permute-start.2
  12.1 1.2 %collective-permute-done.2 = f32[128,128]{1,0:T(8,128)S(1)} collective-permute-done((f32[128,128]{1,0:T(8,128)S(1)}, f32[128,128]{1,0:T(8,128)S(1)}, u32[]{:S(2)}, u32[]{:S(2)}) %collective-permute-start.2) | collective-permute-done | bytes 65568 | tf_op jit(solution)/shard_map/chip_gram/ppermute | solution.py:193
  13.4 1.6 %collective-permute-start.3 = (f32[128,128]{1,0:T(8,128)S(1)}, f32[128,128]{1,0:T(8,128)S(1)}, u32[]{:S(2)}, u32[]{:S(2)}) collective-permute-start(f32[128,128]{1,0:T(8,128)S(1)} %add.10.refs_0_), channel_id=1, source_target_pairs={{0,16},{4,20},{8,24},{12,28},{16,0},{20,4},{24,8},{28,12},{1,17},{... | collective-permute-start | bytes 196616 | tf_op jit(solution)/shard_map/all_gram/ppermute | solution.py:197
  14.9 0.0 collective-permute-done.5
  15.0 1.6 %collective-permute-start.7 = (f32[25,8,128]{2,1,0:T(8,128)S(1)}, f32[25,8,128]{2,1,0:T(8,128)S(1)}, u32[]{:S(2)}, u32[]{:S(2)}) collective-permute-start(f32[25,8,128]{2,1,0:T(8,128)S(1)} %add.11.mine), channel_id=1, source_target_pairs={{0,1},{1,0},{2,3},{3,2},{4,5},{5,4},{6,7},{7,6},{8,9},{9,8},{10,11... | collective-permute-start | bytes 307208 | tf_op jit(solution)/shard_map/other_half/ppermute | solution.py:193
  16.6 0.0 collective-permute-start.6
  16.6 1.1 %collective-permute-done.3.refs_1_ = f32[128,128]{1,0:T(8,128)S(1)} collective-permute-done((f32[128,128]{1,0:T(8,128)S(1)}, f32[128,128]{1,0:T(8,128)S(1)}, u32[]{:S(2)}, u32[]{:S(2)}) %collective-permute-start.3) | collective-permute-done | bytes 65568 | tf_op jit(solution)/shard_map/all_gram/ppermute | solution.py:197
  17.7 0.0 collective-permute-done.4.refs_1_
  17.7 2.0 %collective-permute-done.7.other = f32[25,8,128]{2,1,0:T(8,128)S(1)} collective-permute-done((f32[25,8,128]{2,1,0:T(8,128)S(1)}, f32[25,8,128]{2,1,0:T(8,128)S(1)}, u32[]{:S(2)}, u32[]{:S(2)}) %collective-permute-start.7) | collective-permute-done | bytes 102432 | tf_op jit(solution)/shard_map/other_half/ppermute | solution.py:193
  19.8 0.0 collective-permute-done.6.refs_3_
  19.8 2.7 %solve.1 = f32[24,128]{1,0:T(8,128)} custom-call(f32[512,128]{1,0:T(8,128)S(1)} %copy-done, f32[512,128]{1,0:T(8,128)S(1)} %collective-permute-done.4.refs_1_, f32[512,128]{1,0:T(8,128)S(1)} %collective-permute-done.second.refs_2_, f32[512,128]{1,0:T(8,128)S(1)} %collective-permute-done.6.refs_3_, bf16[128,256]{1,0:T(8,128)(2,1)S(1)} %base.1.refs_4_, ...), custom_call_target="tpu_custom_call" | custom-call | tf_op jit(solution)/shard_map/solve/pallas_call | solution.py:275
  (6 shorter events, 0.1 us)
Async XLA Ops:
  0.0 11.6 %copy-start = (f32[512,128]{1,0:T(8,128)S(1)}, f32[512,128]{1,0:T(8,128)}, u32[]{:S(2)}) copy-start(f32[512,128]{1,0:T(8,128)} %refs_0_.3) | copy-start | bytes 786436
  0.0 11.6 %collective-permute-start = (f32[512,128]{1,0:T(8,128)}, f32[512,128]{1,0:T(8,128)S(1)}, u32[]{:S(2)}, u32[]{:S(2)}) collective-permute-start(f32[512,128]{1,0:T(8,128)} %refs_0_.3), channel_id=1, source_target_pairs={{0,8},{4,12},{8,16},{12,20},{16,24},{20,28},{24,0},{28,4},{1,9},{5... | collective-permute-start | bytes 786440 | tf_op jit(solution)/shard_map/second_shard/ppermute | solution.py:197
  4.2 4.7 %collective-permute-start.1 = (f32[25,8,128]{2,1,0:T(8,128)S(1)}, f32[25,8,128]{2,1,0:T(8,128)S(1)}, u32[]{:S(2)}, u32[]{:S(2)}) collective-permute-start(f32[25,8,128]{2,1,0:T(8,128)S(1)} %get-tuple-element.17), channel_id=1, source_target_pairs={{0,1},{1,0},{2,3},{3,2},{4,5},{5,4},{6,7},{7,6},{8,9},{9,8},{10,11... | collective-permute-start | bytes 307208 | tf_op jit(solution)/shard_map/near_halves/ppermute | solution.py:193
  5.9 11.8 %collective-permute-start.4 = (f32[512,128]{1,0:T(8,128)}, f32[512,128]{1,0:T(8,128)S(1)}, u32[]{:S(2)}, u32[]{:S(2)}) collective-permute-start(f32[512,128]{1,0:T(8,128)} %refs_0_.3), channel_id=1, source_target_pairs={{0,4},{4,16},{8,12},{12,24},{16,20},{20,0},{24,28},{28,8},{1,5},{5... | collective-permute-start | bytes 786440 | tf_op jit(solution)/shard_map/first_shard/ppermute | solution.py:223
  9.0 6.0 %collective-permute-start.5 = (f32[25,8,128]{2,1,0:T(8,128)S(1)}, f32[25,8,128]{2,1,0:T(8,128)S(1)}, u32[]{:S(2)}, u32[]{:S(2)}) collective-permute-start(f32[25,8,128]{2,1,0:T(8,128)S(1)} %add.9), channel_id=1, source_target_pairs={{0,2},{1,3},{2,0},{3,1},{4,6},{5,7},{6,4},{7,5},{8,10},{9,11},{10,... | collective-permute-start | bytes 307208 | tf_op jit(solution)/shard_map/far_halves/ppermute | solution.py:197
  12.0 1.3 %collective-permute-start.2 = (f32[128,128]{1,0:T(8,128)S(1)}, f32[128,128]{1,0:T(8,128)S(1)}, u32[]{:S(2)}, u32[]{:S(2)}) collective-permute-start(f32[128,128]{1,0:T(8,128)S(1)} %gram.1), channel_id=1, source_target_pairs={{0,4},{4,0},{8,12},{12,8},{16,20},{20,16},{24,28},{28,24},{1,5},{5... | collective-permute-start | bytes 196616 | tf_op jit(solution)/shard_map/chip_gram/ppermute | solution.py:193
  13.4 4.3 %collective-permute-start.3 = (f32[128,128]{1,0:T(8,128)S(1)}, f32[128,128]{1,0:T(8,128)S(1)}, u32[]{:S(2)}, u32[]{:S(2)}) collective-permute-start(f32[128,128]{1,0:T(8,128)S(1)} %add.10.refs_0_), channel_id=1, source_target_pairs={{0,16},{4,20},{8,24},{12,28},{16,0},{20,4},{24,8},{28,12},{1,17},{... | collective-permute-start | bytes 196616 | tf_op jit(solution)/shard_map/all_gram/ppermute | solution.py:197
  15.0 4.7 %collective-permute-start.7 = (f32[25,8,128]{2,1,0:T(8,128)S(1)}, f32[25,8,128]{2,1,0:T(8,128)S(1)}, u32[]{:S(2)}, u32[]{:S(2)}) collective-permute-start(f32[25,8,128]{2,1,0:T(8,128)S(1)} %add.11.mine), channel_id=1, source_target_pairs={{0,1},{1,0},{2,3},{3,2},{4,5},{5,4},{6,7},{7,6},{8,9},{9,8},{10,11... | collective-permute-start | bytes 307208 | tf_op jit(solution)/shard_map/other_half/ppermute | solution.py:193
  16.6 3.1 %collective-permute-start.6 = (f32[512,128]{1,0:T(8,128)S(1)}, f32[512,128]{1,0:T(8,128)S(1)}, u32[]{:S(2)}, u32[]{:S(2)}) collective-permute-start(f32[512,128]{1,0:T(8,128)S(1)} %collective-permute-done.second.refs_2_), channel_id=1, source_target_pairs={{0,4},{4,0},{8,12},{12,8},{16,20},{20,16},{24,28},{28,24},{1,5},{5... | collective-permute-start | bytes 786440 | tf_op jit(solution)/shard_map/third_shard/ppermute | solution.py:193
